TPU v7x, 32 devices: a whole 2x2x4 slice. The times are simulated.
32 devices in a mesh: wide: 8 (over z, y), narrow: 4 (over x, core).
Axes of the slice: x: 2, y: 2, z: 4, core: 2. Of those that a mesh axis runs over, the one named last changes fastest.
Arguments:
- target_states: bfloat16 [8, 2048, 512], P('wide', 'narrow'), may hold values from -6 to 6
- memory: bfloat16 [8, 2048, 512], P('wide', 'narrow'), may hold values from -6 to 6
- target_lengths: int32 [8, 16], P('wide'), may hold values from 1 to 1792, as said below
- source_lengths: int32 [8, 16], P('wide'), may hold values from 1 to 1792, as said below
- self_project: bfloat16 [512, 1536], P(('wide', 'narrow')), may hold values from -0.375 to 0.375
- self_output: bfloat16 [512, 512], P(('wide', 'narrow')), may hold values from -1 to 1
- cross_project: bfloat16 [512, 512], P(('wide', 'narrow')), may hold values from -0.375 to 0.375
- memory_project: bfloat16 [512, 1024], P(('wide', 'narrow')), may hold values from -0.375 to 0.375
- cross_output: bfloat16 [512, 512], P(('wide', 'narrow')), may hold values from -1 to 1
- expand_weight: bfloat16 [512, 2048], P(('wide', 'narrow')), may hold values from -0.25 to 0.25
- contract_weight: bfloat16 [2048, 512], P(('wide', 'narrow')), may hold values from -0.125 to 0.125
- norm_gain: bfloat16 [3, 512], P(None, ('wide', 'narrow')), may hold values from 0.5 to 1.5
- norm_bias: bfloat16 [3, 512], P(None, ('wide', 'narrow')), may hold values from -3 to 3
- out_grad: float32 [8, 2048, 512], P('wide', 'narrow'), may hold values from -6 to 6
Outputs:
- output: float32 [8, 2048, 512], P('wide', 'narrow')
- states_grad: float32 [8, 2048, 512], P('wide', 'narrow')
- memory_grad: float32 [8, 2048, 512], P('wide', 'narrow')
- self_project_grad: float32 [512, 1536], P(('wide', 'narrow'))
- self_output_grad: float32 [512, 512], P(('wide', 'narrow'))
- cross_project_grad: float32 [512, 512], P(('wide', 'narrow'))
- memory_project_grad: float32 [512, 1024], P(('wide', 'narrow'))
- cross_output_grad: float32 [512, 512], P(('wide', 'narrow'))
- expand_grad: float32 [512, 2048], P(('wide', 'narrow'))
- contract_grad: float32 [2048, 512], P(('wide', 'narrow'))
- norm_gain_grad: float32 [3, 512], P(None, ('wide', 'narrow'))
- norm_bias_grad: float32 [3, 512], P(None, ('wide', 'narrow'))
Inputs may be any that keep to these rules, and one draw needn't show every extreme that they name: `target_lengths`: each row's 16 sentence lengths are at least 1 and sum to less than 2048; the rest of the row is padding. `source_lengths`: each row's 16 sentence lengths are at least 1 and sum to less than 2048; the rest of the row is padding.
All inputs are finite; a program needn't handle non-finite values.
Results may differ from a plain program's by a relative error of at most 0.025.
The roundings to bfloat16 on the way count: a program that leaves them out, or rounds other values in their place, can miss the bound.
Values may be sent and summed in bfloat16 or wider, within the bound.
No kernel may reach another device: no remote copies, remote signals or barrier semaphores. Data moves between devices by JAX's collectives and lax.ppermute only.
A program may use at most 128 MiB of HBM per device.

v0:
```python
import jax
import jax.numpy as jnp
from jax import lax
from jax.sharding import PartitionSpec as P

HEAD_DIM = 64


ln_eps = 1e-05
masked_score = -1000000000.0


def segment_numbers(lengths, row_span):
    segment_ends = jnp.cumsum(lengths, axis=1)
    position = lax.broadcasted_iota(jnp.int32, (1, row_span, 1), 1)
    return jnp.sum((position >= segment_ends[:, None, :]).astype(jnp.int32), axis=2)


def layer_norm(states, gain_row, offset):
    centred = states - jnp.mean(states, axis=-1, keepdims=True)
    spread = jnp.mean(centred * centred, axis=-1, keepdims=True)
    return centred * lax.rsqrt(spread + ln_eps) * gain_row + offset


def split_heads(tensor):
    row_count, token_count, feature_width = tensor.shape
    return tensor.reshape(row_count, token_count, feature_width // HEAD_DIM, HEAD_DIM).transpose(
        2, 0, 1, 3
    )


def merge_heads(tensor):
    head_count, row_count, token_count, head_width = tensor.shape
    return tensor.transpose(1, 2, 0, 3).reshape(row_count, token_count, head_count * head_width)


def attend_forward(queries, key_block, value_block, allowed):
    score_scale = HEAD_DIM ** (-0.5)

    def one_head(head_items):
        query_head, key_head, value_head = head_items
        raw_scores = jnp.einsum(
            "rqd,rkd->rqk", query_head, key_head, preferred_element_type=jnp.float32
        )
        scaled = jnp.where(allowed, raw_scores * score_scale, masked_score)
        peak_score = jnp.max(scaled, axis=2, keepdims=True)
        weights = jnp.exp(scaled - peak_score)
        totals = jnp.sum(weights, axis=2, keepdims=True)
        prob_low = (weights / totals).astype(jnp.bfloat16)
        mixture = jnp.einsum(
            "rqk,rkd->rqd", prob_low, value_head, preferred_element_type=jnp.float32
        )
        return (mixture, (peak_score + jnp.log(totals))[:, :, 0])

    return lax.map(one_head, (queries, key_block, value_block))


def attend_backward(queries, key_block, value_block, allowed, log_totals, mix_grad):
    score_scale = HEAD_DIM ** (-0.5)

    def one_head(head_items):
        query_head, key_head, value_head, log_head, grad_head = head_items
        raw_scores = jnp.einsum(
            "rqd,rkd->rqk", query_head, key_head, preferred_element_type=jnp.float32
        )
        scaled = jnp.where(allowed, raw_scores * score_scale, masked_score)
        probs_full = jnp.exp(scaled - log_head[:, :, None])
        prob_grad = jnp.einsum(
            "rqd,rkd->rqk", grad_head, value_head, preferred_element_type=jnp.float32
        )
        inner_sum = jnp.sum(probs_full * prob_grad, axis=2, keepdims=True)
        score_grad = (probs_full * (prob_grad - inner_sum) * score_scale).astype(jnp.bfloat16)
        query_grad = jnp.einsum(
            "rqk,rkd->rqd", score_grad, key_head, preferred_element_type=jnp.float32
        )
        key_grad = jnp.einsum(
            "rqk,rqd->rkd", score_grad, query_head, preferred_element_type=jnp.float32
        )
        value_grad = jnp.einsum(
            "rqk,rqd->rkd",
            probs_full.astype(jnp.bfloat16),
            grad_head,
            preferred_element_type=jnp.float32,
        )
        return (query_grad, key_grad, value_grad)

    return lax.map(one_head, (queries, key_block, value_block, log_totals, mix_grad))


def fetch_weights(
    self_project,
    self_output,
    cross_project,
    memory_project,
    cross_output,
    expand_weight,
    contract_weight,
    norm_gain,
    norm_bias,
):
    return (
        lax.all_gather(self_project, ("wide", "narrow"), axis=0, tiled=True),
        lax.all_gather(self_output, ("wide", "narrow"), axis=0, tiled=True),
        lax.all_gather(cross_project, ("wide", "narrow"), axis=0, tiled=True),
        lax.all_gather(memory_project, ("wide", "narrow"), axis=0, tiled=True),
        lax.all_gather(cross_output, ("wide", "narrow"), axis=0, tiled=True),
        lax.all_gather(expand_weight, ("wide", "narrow"), axis=0, tiled=True),
        lax.all_gather(contract_weight, ("wide", "narrow"), axis=0, tiled=True),
        lax.all_gather(norm_gain, ("wide", "narrow"), axis=1, tiled=True),
        lax.all_gather(norm_bias, ("wide", "narrow"), axis=1, tiled=True),
    )


def settle_grads(
    project_grad,
    output_grad,
    cross_grad,
    memory_proj_grad,
    cross_out_grad,
    expand_grad,
    contract_grad,
    gain_grad,
    offset_grad,
):
    return (
        lax.psum_scatter(project_grad, ("wide", "narrow"), scatter_dimension=0, tiled=True),
        lax.psum_scatter(output_grad, ("wide", "narrow"), scatter_dimension=0, tiled=True),
        lax.psum_scatter(cross_grad, ("wide", "narrow"), scatter_dimension=0, tiled=True),
        lax.psum_scatter(memory_proj_grad, ("wide", "narrow"), scatter_dimension=0, tiled=True),
        lax.psum_scatter(cross_out_grad, ("wide", "narrow"), scatter_dimension=0, tiled=True),
        lax.psum_scatter(expand_grad, ("wide", "narrow"), scatter_dimension=0, tiled=True),
        lax.psum_scatter(contract_grad, ("wide", "narrow"), scatter_dimension=0, tiled=True),
        lax.psum_scatter(gain_grad, ("wide", "narrow"), scatter_dimension=1, tiled=True),
        lax.psum_scatter(offset_grad, ("wide", "narrow"), scatter_dimension=1, tiled=True),
    )


def per_device(
    target_states,
    memory,
    target_lengths,
    source_lengths,
    self_project,
    self_output,
    cross_project,
    memory_project,
    cross_output,
    expand_weight,
    contract_weight,
    norm_gain,
    norm_bias,
    out_grad,
):
    row_count, local_len, model_width = target_states.shape
    source_local = memory.shape[1]
    narrow_size = lax.axis_size("narrow")
    narrow_index = lax.axis_index("narrow")
    target_ids = segment_numbers(target_lengths, local_len * narrow_size)
    source_ids = segment_numbers(source_lengths, source_local * narrow_size)
    own_ids = lax.dynamic_slice_in_dim(target_ids, narrow_index * local_len, local_len, 1)
    self_allowed = own_ids[:, :, None] == target_ids[:, None, :]
    cross_allowed = own_ids[:, :, None] == source_ids[:, None, :]
    (
        self_whole,
        sout_whole,
        cproj_whole,
        mproj_whole,
        cout_whole,
        expand_whole,
        contract_whole,
        gain_whole,
        offset_whole,
    ) = fetch_weights(
        self_project,
        self_output,
        cross_project,
        memory_project,
        cross_output,
        expand_weight,
        contract_weight,
        norm_gain,
        norm_bias,
    )
    gain_rows = gain_whole.astype(jnp.float32)
    offset_rows = offset_whole.astype(jnp.float32)
    query_low = jnp.dot(
        target_states, self_whole[:, :model_width], preferred_element_type=jnp.float32
    ).astype(jnp.bfloat16)
    pair_low = jnp.dot(
        target_states, self_whole[:, model_width:], preferred_element_type=jnp.float32
    ).astype(jnp.bfloat16)
    pair_rows = lax.all_gather(pair_low, "narrow", axis=1, tiled=True)
    key_part = pair_rows[:, :, :model_width]
    value_part = pair_rows[:, :, model_width:]
    self_query = split_heads(query_low)
    self_key = split_heads(key_part)
    self_value = split_heads(value_part)
    self_mixture, self_logs = attend_forward(self_query, self_key, self_value, self_allowed)
    self_mix = merge_heads(self_mixture).astype(jnp.bfloat16)
    states_float = target_states.astype(jnp.float32)
    first_norm, first_pull = jax.vjp(
        layer_norm,
        states_float + jnp.dot(self_mix, sout_whole, preferred_element_type=jnp.float32),
        gain_rows[0],
        offset_rows[0],
    )
    first_low = first_norm.astype(jnp.bfloat16)
    cross_low = jnp.dot(first_low, cproj_whole, preferred_element_type=jnp.float32).astype(
        jnp.bfloat16
    )
    memory_pairs = jnp.dot(memory, mproj_whole, preferred_element_type=jnp.float32).astype(
        jnp.bfloat16
    )
    memory_rows = lax.all_gather(memory_pairs, "narrow", axis=1, tiled=True)
    mkey_part = memory_rows[:, :, :model_width]
    mvalue_part = memory_rows[:, :, model_width:]
    cross_query = split_heads(cross_low)
    cross_key = split_heads(mkey_part)
    cross_value = split_heads(mvalue_part)
    cross_mixture, cross_logs = attend_forward(cross_query, cross_key, cross_value, cross_allowed)
    cross_mix = merge_heads(cross_mixture).astype(jnp.bfloat16)
    second_norm, second_pull = jax.vjp(
        layer_norm,
        first_norm + jnp.dot(cross_mix, cout_whole, preferred_element_type=jnp.float32),
        gain_rows[1],
        offset_rows[1],
    )
    second_low = second_norm.astype(jnp.bfloat16)
    forward_hidden = jnp.dot(second_low, expand_whole, preferred_element_type=jnp.float32)
    forward_active = jax.nn.gelu(forward_hidden).astype(jnp.bfloat16)
    output, third_pull = jax.vjp(
        layer_norm,
        second_norm + jnp.dot(forward_active, contract_whole, preferred_element_type=jnp.float32),
        gain_rows[2],
        offset_rows[2],
    )
    (
        self_whole,
        sout_whole,
        cproj_whole,
        mproj_whole,
        cout_whole,
        expand_whole,
        contract_whole,
        gain_whole,
        offset_whole,
    ) = fetch_weights(
        self_project,
        self_output,
        cross_project,
        memory_project,
        cross_output,
        expand_weight,
        contract_weight,
        norm_gain,
        norm_bias,
    )
    third_grad, gain_three, offset_three = third_pull(out_grad)
    ffn_grad = third_grad.astype(jnp.bfloat16)
    hidden = jnp.dot(second_low, expand_whole, preferred_element_type=jnp.float32)
    active = jax.nn.gelu(hidden).astype(jnp.bfloat16)
    contract_grad = jnp.einsum("rnf,rnd->fd", active, ffn_grad, preferred_element_type=jnp.float32)
    active_grad = jnp.dot(ffn_grad, contract_whole.T, preferred_element_type=jnp.float32)
    hidden_grad = jax.vjp(jax.nn.gelu, hidden)[1](active_grad)[0].astype(jnp.bfloat16)
    expand_grad = jnp.einsum(
        "rnd,rnf->df", second_low, hidden_grad, preferred_element_type=jnp.float32
    )
    second_grad, gain_two, offset_two = second_pull(
        third_grad + jnp.dot(hidden_grad, expand_whole.T, preferred_element_type=jnp.float32)
    )
    cross_out_low = second_grad.astype(jnp.bfloat16)
    cross_out_grad = jnp.einsum(
        "rnc,rnd->cd", cross_mix, cross_out_low, preferred_element_type=jnp.float32
    )
    cross_mix_grad = jnp.dot(
        cross_out_low, cout_whole.T, preferred_element_type=jnp.float32
    ).astype(jnp.bfloat16)
    cross_query_grad, cross_key_grad, cross_value_grad = attend_backward(
        cross_query, cross_key, cross_value, cross_allowed, cross_logs, split_heads(cross_mix_grad)
    )
    memory_terms = jnp.concatenate(
        [merge_heads(cross_key_grad), merge_heads(cross_value_grad)], axis=2
    )
    memory_pair_grad = lax.psum_scatter(
        memory_terms.astype(jnp.bfloat16), "narrow", scatter_dimension=1, tiled=True
    )
    cross_query_low = merge_heads(cross_query_grad).astype(jnp.bfloat16)
    memory_proj_grad = jnp.einsum(
        "rsd,rse->de", memory, memory_pair_grad, preferred_element_type=jnp.float32
    )
    memory_grad = jnp.dot(memory_pair_grad, mproj_whole.T, preferred_element_type=jnp.float32)
    cross_proj_grad = jnp.einsum(
        "rnd,rne->de", first_low, cross_query_low, preferred_element_type=jnp.float32
    )
    first_grad, gain_one, offset_one = first_pull(
        second_grad + jnp.dot(cross_query_low, cproj_whole.T, preferred_element_type=jnp.float32)
    )
    self_out_low = first_grad.astype(jnp.bfloat16)
    self_out_grad = jnp.einsum(
        "rnc,rnd->cd", self_mix, self_out_low, preferred_element_type=jnp.float32
    )
    self_mix_grad = jnp.dot(self_out_low, sout_whole.T, preferred_element_type=jnp.float32).astype(
        jnp.bfloat16
    )
    self_query_grad, self_key_grad, self_value_grad = attend_backward(
        self_query, self_key, self_value, self_allowed, self_logs, split_heads(self_mix_grad)
    )
    pair_terms = jnp.concatenate([merge_heads(self_key_grad), merge_heads(self_value_grad)], axis=2)
    pair_grad = lax.psum_scatter(
        pair_terms.astype(jnp.bfloat16), "narrow", scatter_dimension=1, tiled=True
    )
    packed_grad = jnp.concatenate(
        [merge_heads(self_query_grad).astype(jnp.bfloat16), pair_grad], axis=2
    )
    self_proj_grad = jnp.einsum(
        "rnd,rne->de", target_states, packed_grad, preferred_element_type=jnp.float32
    )
    states_grad = first_grad + jnp.dot(
        packed_grad, self_whole.T, preferred_element_type=jnp.float32
    )
    gain_grad = jnp.stack([gain_one, gain_two, gain_three])
    offset_grad = jnp.stack([offset_one, offset_two, offset_three])
    settled = settle_grads(
        self_proj_grad,
        self_out_grad,
        cross_proj_grad,
        memory_proj_grad,
        cross_out_grad,
        expand_grad,
        contract_grad,
        gain_grad,
        offset_grad,
    )
    return (
        output,
        states_grad,
        memory_grad,
        settled[0],
        settled[1],
        settled[2],
        settled[3],
        settled[4],
        settled[5],
        settled[6],
        settled[7],
        settled[8],
    )


def solution(mesh):
    in_specs = (
        P("wide", "narrow", None),
        P("wide", "narrow", None),
        P("wide", None),
        P("wide", None),
        P(("wide", "narrow"), None),
        P(("wide", "narrow"), None),
        P(("wide", "narrow"), None),
        P(("wide", "narrow"), None),
        P(("wide", "narrow"), None),
        P(("wide", "narrow"), None),
        P(("wide", "narrow"), None),
        P(None, ("wide", "narrow")),
        P(None, ("wide", "narrow")),
        P("wide", "narrow", None),
    )
    out_specs = (
        P("wide", "narrow", None),
        P("wide", "narrow", None),
        P("wide", "narrow", None),
        P(("wide", "narrow"), None),
        P(("wide", "narrow"), None),
        P(("wide", "narrow"), None),
        P(("wide", "narrow"), None),
        P(("wide", "narrow"), None),
        P(("wide", "narrow"), None),
        P(("wide", "narrow"), None),
        P(None, ("wide", "narrow")),
        P(None, ("wide", "narrow")),
    )
    return jax.shard_map(
        per_device, mesh=mesh, in_specs=in_specs, out_specs=out_specs, check_vma=False
    )
```

profile of v0, /device:TPU:0, one launch (start us, length us, event | category | flops | bytes accessed | tf_op | source)
XLA Modules:
  0.0 1922.6 jit_solution(16033391699682418231)
XLA Ops:
  8.8 58.5 %all-gather.13.cloned.1.call-done = bf16[512,1024]{1,0:T(8,128)(2,1)} async-done(((bf16[16,1024]{1,0:T(8,128)(2,1)}), bf16[512,1024]{1,0:T(8,128)(2,1)}) %all-gather.13.cloned.1.call-update) | async-done | bytes 1048592 | tf_op jit(solution)/shard_map/all_gather | solution.py:105
  67.3 3.0 convolution_convert_fusion
  70.4 53.7 %all-gather.11.cloned.1.call-done = bf16[512,1536]{1,0:T(8,128)(2,1)} async-done(((bf16[16,1536]{1,0:T(8,128)(2,1)}), bf16[512,1536]{1,0:T(8,128)(2,1)}) %all-gather.11.cloned.1.call-update) | async-done | bytes 1572880 | tf_op jit(solution)/shard_map/all_gather | solution.py:102
  124.1 3.1 convolution_convert_fusion.1
  130.0 39.5 %all-gather.2 = bf16[32,16,3]{1,2,0:T(4,128)(2,1)S(1)} all-gather(bf16[1,16,3]{1,2,0:T(4,128)(2,1)S(1)} %bitcast.423), channel_id=1, replica_groups=mesh['wide'=8,'narrow'=4] {'wide','narrow'}, dimensions={0}, use_global_device_ids=true | all-gather | bytes 3168 | tf_op jit(solution)/shard_map/all_gather | solution.py:109
  169.5 36.7 %all-gather.3 = bf16[32,16,3]{1,2,0:T(4,128)(2,1)S(1)} all-gather(bf16[1,16,3]{1,2,0:T(4,128)(2,1)S(1)} %bitcast.424), channel_id=1, replica_groups=mesh['wide'=8,'narrow'=4] {'wide','narrow'}, dimensions={0}, use_global_device_ids=true | all-gather | bytes 3168 | tf_op jit(solution)/shard_map/all_gather | solution.py:110
  206.7 39.7 %all_gather.42 = bf16[512,512]{1,0:T(8,128)(2,1)S(1)} all-gather(bf16[16,512]{1,0:T(8,128)(2,1)S(1)} %copy-done.22), channel_id=1, replica_groups=mesh['wide'=8,'narrow'=4] {'wide','narrow'}, dimensions={0}, use_global_device_ids=true | all-gather | bytes 540672 | tf_op jit(solution)/shard_map/all_gather | solution.py:103
  246.4 41.4 %all_gather.45 = bf16[512,512]{1,0:T(8,128)(2,1)} all-gather(bf16[16,512]{1,0:T(8,128)(2,1)S(1)} %copy-done.23), channel_id=1, replica_groups=mesh['wide'=8,'narrow'=4] {'wide','narrow'}, dimensions={0}, use_global_device_ids=true | all-gather | bytes 540672 | tf_op jit(solution)/shard_map/all_gather | solution.py:104
  287.8 42.7 %all_gather.48 = bf16[512,512]{1,0:T(8,128)(2,1)} all-gather(bf16[16,512]{1,0:T(8,128)(2,1)S(1)} %copy-done.24), channel_id=1, replica_groups=mesh['wide'=8,'narrow'=4] {'wide','narrow'}, dimensions={0}, use_global_device_ids=true | all-gather | bytes 540672 | tf_op jit(solution)/shard_map/all_gather | solution.py:106
  334.7 4.5 fusion.138
  339.3 2.9 copy.140
  342.2 3.2 copy.142
  345.4 2.9 copy.139
  348.3 3.2 copy.141
  351.5 4.5 fusion.139
  356.1 2.9 copy.131
  359.0 3.2 copy.133
  362.2 2.9 copy.130
  365.1 3.2 copy.132
  368.4 38.8 %while.56 = (s32[]{:T(128)}, bf16[8,1,512,64]{2,3,1,0:T(8,128)(2,1)S(1)}, f32[8,1,512]{2,1,0:T(1,128)S(1)}, bf16[8,1,512,64]{3,2,1,0:T(8,128)(2,1)}, bf16[8,1,20...) while((s32[]{:T(128)}, ...), condition=%wide.region_5.6_spmd.clone, body=%wide.region_2.0_spmd.clone.sunk | while | flops 277872128 | bytes 13926505 | solution.py:55
  411.1 43.1 %while.57 = (s32[]{:T(128)}, bf16[8,1,512,64]{2,3,1,0:T(8,128)(2,1)}, f32[8,1,512]{2,1,0:T(1,128)S(1)}, bf16[8,1,512,64]{3,2,1,0:T(8,128)(2,1)S(1)}, bf16[8,1,20...) while((s32[]{:T(128)}, ...), condition=%wide.region_13.14_spmd.clone, body=%wide.region_10.13_spmd.clone.sunk | while | flops 277872128 | bytes 13926505 | solution.py:55
  413.8 2.7 fusion.209
  419.2 2.7 fusion.209
  424.5 2.7 fusion.209
  429.9 2.7 fusion.209
  435.2 2.7 fusion.209
  440.6 2.7 fusion.209
  446.0 2.7 fusion.209
  451.3 2.7 fusion.209
  457.0 4.9 fusion.128
  461.9 4.9 fusion.144
  470.5 3.7 fusion.86
  484.1 89.3 %while.58 = (s32[]{:T(128)}, bf16[8,1,512,64]{2,3,1,0:T(8,128)(2,1)S(1)}, bf16[8,1,2048,64]{2,3,1,0:T(8,128)(2,1)}, bf16[8,1,2048,64]{2,3,1,0:T(8,128)(2,1)}, bf...) while((s32[]{:T(128)}, ...), condition=%wide.region_24.25_spmd.clone, body=%wide.region_22.24_spmd.clone.sunk | while | flops 682622464 | bytes 34759808 | solution.py:87
  486.2 2.6 multiply_reduce_fusion.13
  497.3 2.6 multiply_reduce_fusion.13
  508.4 2.6 multiply_reduce_fusion.13
  519.6 2.6 multiply_reduce_fusion.13
  530.7 2.6 multiply_reduce_fusion.13
  541.9 2.6 multiply_reduce_fusion.13
  553.0 2.6 multiply_reduce_fusion.13
  564.1 2.6 multiply_reduce_fusion.13
  573.4 4.8 pad_maximum_fusion.1
  589.5 94.0 %while.59 = (s32[]{:T(128)}, bf16[8,1,512,64]{2,3,1,0:T(8,128)(2,1)}, bf16[8,1,2048,64]{2,3,1,0:T(8,128)(2,1)}, bf16[8,1,2048,64]{2,3,1,0:T(8,128)(2,1)}, bf16[8...) while((s32[]{:T(128)}, ...), condition=%wide.region_29.30_spmd.clone, body=%wide.region_27.29_spmd.clone.sunk | while | flops 682622464 | bytes 34759808 | solution.py:87
  603.1 2.6 multiply_reduce_fusion.14
  683.5 4.8 pad_maximum_fusion
  693.1 3.3 fusion.112
  698.3 6.4 fusion.115
  704.7 4.8 fusion.126
  709.7 3.4 convolution_bitcast_fusion.7
  713.1 2.9 copy.163
  716.0 13.2 reduce-scatter.20.cloned.1.call-done
  729.3 4.0 convolution_bitcast_fusion.6
  733.3 3.7 copy.161
  738.3 126.7 %reduce-scatter.40.cloned.1.call-done = f32[16,3]{1,0:T(8,128)} async-done(((f32[512,3]{1,0:T(8,128)}), f32[16,3]{1,0:T(8,128)}) %reduce-scatter.40.cloned.1.call-update) | async-done | bytes 208
  866.4 130.8 %reduce-scatter.38.cloned.1.call-done = f32[16,3]{1,0:T(8,128)} async-done(((f32[512,3]{1,0:T(8,128)}), f32[16,3]{1,0:T(8,128)}) %reduce-scatter.38.cloned.1.call-update) | async-done | bytes 208
  998.5 3.7 fusion.92
  1004.7 2.9 convolution_bitcast_fusion.10
  1007.7 123.0 %reduce-scatter.26.cloned.1.call-done = f32[16,512]{1,0:T(8,128)} async-done(((f32[512,512]{1,0:T(8,128)}), f32[16,512]{1,0:T(8,128)}) %reduce-scatter.26.cloned.1.call-update) | async-done | bytes 32784 | tf_op jit(solution)/shard_map/reduce_scatter | solution.py:128
  1130.7 133.5 %reduce-scatter.28.cloned.1.call-done = f32[16,512]{1,0:T(8,128)} async-done(((f32[512,512]{1,0:T(8,128)}), f32[16,512]{1,0:T(8,128)}) %reduce-scatter.28.cloned.1.call-update) | async-done | bytes 32784 | tf_op jit(solution)/shard_map/reduce_scatter | solution.py:130
  1264.2 133.6 %reduce-scatter.24.cloned.1.call-done = f32[16,512]{1,0:T(8,128)} async-done(((f32[512,512]{1,0:T(8,128)}), f32[16,512]{1,0:T(8,128)}) %reduce-scatter.24.cloned.1.call-update) | async-done | bytes 32784 | tf_op jit(solution)/shard_map/reduce_scatter | solution.py:127
  1397.8 139.7 %reduce-scatter.32.cloned.1.call-done = f32[64,512]{1,0:T(8,128)} async-done(((f32[2048,512]{1,0:T(8,128)}), f32[64,512]{1,0:T(8,128)}) %reduce-scatter.32.cloned.1.call-update) | async-done | bytes 131088 | tf_op jit(solution)/shard_map/reduce_scatter | solution.py:132
  1537.5 139.5 %reduce-scatter.30.cloned.1.call-done = f32[16,2048]{1,0:T(8,128)} async-done(((f32[512,2048]{1,0:T(8,128)}), f32[16,2048]{1,0:T(8,128)}) %reduce-scatter.30.cloned.1.call-update) | async-done | bytes 131088 | tf_op jit(solution)/shard_map/reduce_scatter | solution.py:131
  1677.0 135.3 %reduce-scatter.36.cloned.1.call-done = f32[16,1024]{1,0:T(8,128)} async-done(((f32[512,1024]{1,0:T(8,128)}), f32[16,1024]{1,0:T(8,128)}) %reduce-scatter.36.cloned.1.call-update) | async-done | bytes 65552
  1812.4 103.4 %reduce-scatter.34.cloned.1.call-done = f32[16,1536]{1,0:T(8,128)} async-done(((f32[512,1536]{1,0:T(8,128)}), f32[16,1536]{1,0:T(8,128)}) %reduce-scatter.34.cloned.1.call-update) | async-done | bytes 98320
  (341 shorter events, 272.6 us)
Async XLA Ops:
  7.2 60.1 %copy-start = (bf16[1,512,512]{2,1,0:T(8,128)(2,1)S(1)}, bf16[1,512,512]{2,1,0:T(8,128)(2,1)}, u32[]{:S(2)}) copy-start(bf16[1,512,512]{2,1,0:T(8,128)(2,1)} %param.23) | copy-start | bytes 1572868
  7.2 60.1 %all-gather.13.cloned.1.call-start = ((), (), s32[]{:S(2)}) async-start(), calls=%async_computation.12 | async-start | bytes 1081344 | tf_op jit(solution)/shard_map/all_gather | solution.py:105
  7.9 120.5 %copy-start.20 = (bf16[1,512,512]{2,1,0:T(8,128)(2,1)S(1)}, bf16[1,512,512]{2,1,0:T(8,128)(2,1)}, u32[]{:S(2)}) copy-start(bf16[1,512,512]{2,1,0:T(8,128)(2,1)} %param.22) | copy-start | bytes 1572868
  7.9 116.1 %all-gather.11.cloned.1.call-start = ((), (), s32[]{:S(2)}) async-start(), calls=%async_computation.11 | async-start | bytes 1622016 | tf_op jit(solution)/shard_map/all_gather | solution.py:102
  8.7 120.7 %copy-start.28 = (s32[1,16]{1,0:T(1,128)S(1)}, s32[1,16]{1,0:T(1,128)}, u32[]{:S(2)}) copy-start(s32[1,16]{1,0:T(1,128)} %param.24) | copy-start | bytes 196
  8.7 120.9 %copy-start.29 = (s32[1,16]{1,0:T(1,128)S(1)}, s32[1,16]{1,0:T(1,128)}, u32[]{:S(2)}) copy-start(s32[1,16]{1,0:T(1,128)} %param.25) | copy-start | bytes 196
  8.7 121.3 %copy-start.25 = (bf16[3,16]{1,0:T(4,128)(2,1)S(1)}, bf16[3,16]{1,0:T(4,128)(2,1)}, u32[]{:S(2)}) copy-start(bf16[3,16]{1,0:T(4,128)(2,1)} %param.33) | copy-start | bytes 292
  8.7 160.8 %copy-start.26 = (bf16[3,16]{1,0:T(4,128)(2,1)S(1)}, bf16[3,16]{1,0:T(4,128)(2,1)}, u32[]{:S(2)}) copy-start(bf16[3,16]{1,0:T(4,128)(2,1)} %param.34) | copy-start | bytes 292
  8.7 198.0 %copy-start.22 = (bf16[16,512]{1,0:T(8,128)(2,1)S(1)}, bf16[16,512]{1,0:T(8,128)(2,1)}, u32[]{:S(2)}) copy-start(bf16[16,512]{1,0:T(8,128)(2,1)} %param.27) | copy-start | bytes 49156
  8.7 326.0 %all-gather.21.cloned.1.call-start = ((), (), s32[]{:S(2)}) async-start(), calls=%async_computation.23 | async-start | bytes 5242880 | tf_op jit(solution)/shard_map/all_gather | solution.py:214
  70.3 176.1 %copy-start.23 = (bf16[16,512]{1,0:T(8,128)(2,1)S(1)}, bf16[16,512]{1,0:T(8,128)(2,1)}, u32[]{:S(2)}) copy-start(bf16[16,512]{1,0:T(8,128)(2,1)} %param.28) | copy-start | bytes 49156
  70.3 217.5 %copy-start.24 = (bf16[16,512]{1,0:T(8,128)(2,1)S(1)}, bf16[16,512]{1,0:T(8,128)(2,1)}, u32[]{:S(2)}) copy-start(bf16[16,512]{1,0:T(8,128)(2,1)} %param.30) | copy-start | bytes 49156
  70.3 260.2 %copy-start.13 = (f32[1,512,512]{2,1,0:T(8,128)S(1)}, f32[1,512,512]{2,1,0:T(8,128)}, u32[]{:S(2)}) copy-start(f32[1,512,512]{2,1,0:T(8,128)} %param.35) | copy-start | bytes 3145732
  70.3 281.2 %all-gather.19.cloned.1.call-start = ((), (), s32[]{:S(2)}) async-start(), calls=%async_computation.22 | async-start | bytes 5242880 | tf_op jit(solution)/shard_map/all_gather | solution.py:192
  127.2 329.8 %all-gather.15.cloned.1.call-start = ((), (), s32[]{:S(2)}) async-start(), calls=%async_computation.13 | async-start | bytes 2162688 | tf_op jit(solution)/shard_map/all_gather | solution.py:107
  127.8 334.2 %all-gather.17.cloned.1.call-start = ((), (), s32[]{:S(2)}) async-start(), calls=%async_computation.14 | async-start | bytes 2162688 | tf_op jit(solution)/shard_map/all_gather | solution.py:108
  128.3 581.4 %reduce-scatter.22.cloned.1.call-start = ((), (), s32[]{:S(2)}) async-start(), calls=%async_computation.16 | async-start | bytes 5242880 | tf_op jit(solution)/shard_map/reduce_scatter | solution.py:284
  246.4 160.8 %copy-start.6 = (bf16[512,512]{1,0:T(8,128)(2,1)}, bf16[512,512]{1,0:T(8,128)(2,1)S(1)}, u32[]{:S(2)}) copy-start(bf16[512,512]{1,0:T(8,128)(2,1)S(1)} %all_gather.42) | copy-start | bytes 1572868
  368.4 40.8 %copy-start.14 = (bf16[512,512]{1,0:T(8,128)(2,1)S(1)}, bf16[512,512]{1,0:T(8,128)(2,1)}, u32[]{:S(2)}) copy-start(bf16[512,512]{1,0:T(8,128)(2,1)} %all_gather.45) | copy-start | bytes 1572868
  407.2 2.6 copy-start.9
  411.1 44.1 %copy-start.8 = (bf16[512,512]{1,0:T(8,128)(2,1)S(1)}, bf16[512,512]{1,0:T(8,128)(2,1)}, u32[]{:S(2)}) copy-start(bf16[512,512]{1,0:T(8,128)(2,1)} %all_gather.48) | copy-start | bytes 1572868
  454.2 1.0 copy-start.5
  461.9 5.1 copy-start.2
  466.8 2.6 copy-start.12
  466.9 3.6 copy-start.27
  468.8 5.3 copy-start.17
  470.5 3.7 copy-start.16
  474.2 1.7 copy-start.15
  476.2 1.0 copy-start.1
  578.2 151.1 %reduce-scatter.20.cloned.1.call-start = ((), (), s32[]{:S(2)}) async-start(), calls=%async_computation.15 | async-start | bytes 5242880 | tf_op jit(solution)/shard_map/reduce_scatter | solution.py:309
  578.3 3.6 copy-start.7
  580.8 1.0 copy-start.3
  688.3 176.7 %reduce-scatter.40.cloned.1.call-start = ((), (), s32[]{:S(2)}) async-start(), calls=%async_computation.27 | async-start | bytes 270336
  690.6 306.5 %reduce-scatter.38.cloned.1.call-start = ((), (), s32[]{:S(2)}) async-start(), calls=%async_computation.26 | async-start | bytes 270336
  691.5 439.1 %reduce-scatter.26.cloned.1.call-start = ((), (), s32[]{:S(2)}) async-start(), calls=%async_computation.18 | async-start | bytes 1081344 | tf_op jit(solution)/shard_map/reduce_scatter | solution.py:128
  693.1 3.5 copy-start.4
  693.1 3.5 copy-start.10
  693.1 571.1 %reduce-scatter.28.cloned.1.call-start = ((), (), s32[]{:S(2)}) async-start(), calls=%async_computation.19 | async-start | bytes 1081344 | tf_op jit(solution)/shard_map/reduce_scatter | solution.py:130
  696.5 701.3 %reduce-scatter.24.cloned.1.call-start = ((), (), s32[]{:S(2)}) async-start(), calls=%async_computation.17 | async-start | bytes 1081344 | tf_op jit(solution)/shard_map/reduce_scatter | solution.py:127
  698.0 839.5 %reduce-scatter.32.cloned.1.call-start = ((), (), s32[]{:S(2)}) async-start(), calls=%async_computation.21 | async-start | bytes 4325376 | tf_op jit(solution)/shard_map/reduce_scatter | solution.py:132
  704.7 972.3 %reduce-scatter.30.cloned.1.call-start = ((), (), s32[]{:S(2)}) async-start(), calls=%async_computation.20 | async-start | bytes 4325376 | tf_op jit(solution)/shard_map/reduce_scatter | solution.py:131
  709.6 19.7 %copy-start.19 = (bf16[8,1,512,64]{2,3,1,0:T(8,128)(2,1)S(1)}, bf16[8,1,512,64]{2,3,1,0:T(8,128)(2,1)}, u32[]{:S(2)}) copy-start(bf16[8,1,512,64]{2,3,1,0:T(8,128)(2,1)} %get-tuple-element.201) | copy-start | bytes 1572868
  709.6 19.7 %copy-start.21 = (bf16[1,512,512]{2,1,0:T(8,128)(2,1)S(1)}, bf16[1,512,512]{2,1,0:T(8,128)(2,1)}, u32[]{:S(2)}) copy-start(bf16[1,512,512]{2,1,0:T(8,128)(2,1)} %param.22) | copy-start | bytes 1572868
  709.6 1102.7 %reduce-scatter.36.cloned.1.call-start = ((), (), s32[]{:S(2)}) async-start(), calls=%async_computation.25 | async-start | bytes 2162688
  716.0 1199.8 %reduce-scatter.34.cloned.1.call-start = ((), (), s32[]{:S(2)}) async-start(), calls=%async_computation.24 | async-start | bytes 3244032
  733.3 3.8 copy-start.11
  998.5 6.3 copy-start.18
Sparse Core Ops, SparseCore 0:
  10.9 56.3 all-gather.12
  70.1 53.8 all-gather.10
  125.6 33.6 all-gather.20
  161.3 34.7 all-gather.18
  198.8 57.5 all-gather.14
  259.1 55.5 all-gather.16
  578.3 40.7 reduce-scatter.21
  688.4 40.8 reduce-scatter.19
  731.5 133.4 reduce-scatter.39
  867.8 129.3 reduce-scatter.37
  999.9 130.7 reduce-scatter.25
  1133.4 130.6 reduce-scatter.27
  1267.0 130.7 reduce-scatter.23
  1400.6 136.8 reduce-scatter.31
  1540.3 136.6 reduce-scatter.29
  1679.8 132.5 reduce-scatter.35
  1818.2 97.5 reduce-scatter.33
where the time goes:
time: 1930 us; the launch traced here: 1920 us
  waiting for transfers between devices  1290 us (67%)
  matrix products  307 us (16%)
  blocking collectives  200 us (10%)
  local copies, waits for them, and re-layouts  71 us (4%)
  other arithmetic  34.7 us (2%)
    unnamed x21, waiting for transfers between devices  499 us
    reduce_scatter x1, waiting for transfers between devices, settle_grads(): lax.psum_scatter(contract_grad, ('wide', 'narrow'), scatter_dimension=0,...  140 us
    reduce_scatter x1, waiting for transfers between devices, settle_grads(): lax.psum_scatter(expand_grad, ('wide', 'narrow'), scatter_dimension=0, ti...  140 us
    reduce_scatter x1, waiting for transfers between devices, settle_grads(): lax.psum_scatter(output_grad, ('wide', 'narrow'), scatter_dimension=0, ti...  134 us
    reduce_scatter x1, waiting for transfers between devices, settle_grads(): lax.psum_scatter(cross_out_grad, ('wide', 'narrow'), scatter_dimension=0,...  133 us
    reduce_scatter x1, waiting for transfers between devices, settle_grads(): lax.psum_scatter(cross_grad, ('wide', 'narrow'), scatter_dimension=0, til...  123 us
    dot_general x32, matrix products, one_head(): jnp.einsum('rqd,rkd->rqk', query_head, key_head, preferred_element_type=j...  73.2 us
    all_gather x1, waiting for transfers between devices, fetch_weights(): lax.all_gather(memory_project, ('wide', 'narrow'), axis=0, tiled=True)  58.5 us
  transfers between devices with their start and end apart: 17, of which 12 were waited for; matrix products, arithmetic and copies ran while one was open for 15% of the time, Pallas kernels for 0%

commit v1 on v0

--- a/solution.py
+++ b/solution.py
@@ -85,6 +85,94 @@
         return (query_grad, key_grad, value_grad)
 
     return lax.map(one_head, (queries, key_block, value_block, log_totals, mix_grad))
+
+
+def axis_bits():
+    wide_bits = lax.axis_size("wide").bit_length() - 1
+    narrow_bits = lax.axis_size("narrow").bit_length() - 1
+    return wide_bits, narrow_bits
+
+
+def exchange(block, mask):
+    device_count = lax.axis_size("wide") * lax.axis_size("narrow")
+    pairs = [(device, device ^ mask) for device in range(device_count)]
+    return lax.ppermute(block, ("wide", "narrow"), pairs)
+
+
+def stages():
+    wide_bits, narrow_bits = axis_bits()
+    total = wide_bits + narrow_bits
+    near = list(range(0, narrow_bits - 1))
+    plane = [narrow_bits - 1, narrow_bits]
+    far = list(range(narrow_bits + 1, total))
+    groups = [tuple(far[at : at + 2]) for at in range(0, len(far), 2)][::-1]
+    return groups + [tuple(plane)] + [(bit,) for bit in near]
+
+
+def masks_of(bits):
+    out = []
+    for number in range(2 ** len(bits)):
+        out.append(sum(1 << bit for at, bit in enumerate(bits) if number >> at & 1))
+    return out
+
+
+def device_number():
+    return lax.axis_index("wide") * lax.axis_size("narrow") + lax.axis_index("narrow")
+
+
+def local_number(me, bits):
+    return sum(((me >> bit) & 1) << at for at, bit in enumerate(bits))
+
+
+def gather_shards(shard):
+    me = device_number()
+    wide_bits, narrow_bits = axis_bits()
+    total = wide_bits + narrow_bits
+    held = shard[None]
+    done = []
+    for bits in stages():
+        mine = local_number(me, bits)
+        whole = jnp.zeros((2 ** len(bits),) + held.shape, held.dtype)
+        for number, mask in enumerate(masks_of(bits)):
+            block = held if number == 0 else exchange(held, mask)
+            whole = lax.dynamic_update_slice_in_dim(whole, block[None], mine ^ number, 0)
+        held = whole
+        done = list(bits) + done
+    groups = stages()
+    shape = []
+    order = []
+    for bits in groups[::-1]:
+        for bit in bits[::-1]:
+            shape.append(2)
+            order.append(bit)
+    held = held.reshape(tuple(shape) + shard.shape)
+    places = [order.index(bit) for bit in range(total - 1, -1, -1)]
+    held = held.transpose(tuple(places) + (total, total + 1))
+    return held.reshape((2**total,) + shard.shape)
+
+
+def scatter_sums(terms):
+    me = device_number()
+    wide_bits, narrow_bits = axis_bits()
+    total = wide_bits + narrow_bits
+    groups = stages()
+    order = []
+    for bits in groups[::-1]:
+        order += list(bits[::-1])
+    tail = terms.shape[1:]
+    held = terms.astype(jnp.bfloat16).reshape((2,) * total + tail)
+    places = [total - 1 - bit for bit in order]
+    held = held.transpose(tuple(places) + (total, total + 1))
+    for bits in groups[::-1]:
+        held = held.reshape((2 ** len(bits), -1) + tail)
+        mine = local_number(me, bits)
+        total_sum = lax.dynamic_index_in_dim(held, mine, 0, keepdims=False).astype(jnp.float32)
+        for number, mask in enumerate(masks_of(bits)):
+            if number:
+                block = lax.dynamic_index_in_dim(held, mine ^ number, 0, keepdims=False)
+                total_sum = total_sum + exchange(block, mask).astype(jnp.float32)
+        held = total_sum.astype(jnp.bfloat16)
+    return total_sum[0]
 
 
 def fetch_weights(
@@ -98,17 +186,37 @@
     norm_gain,
     norm_bias,
 ):
-    return (
-        lax.all_gather(self_project, ("wide", "narrow"), axis=0, tiled=True),
-        lax.all_gather(self_output, ("wide", "narrow"), axis=0, tiled=True),
-        lax.all_gather(cross_project, ("wide", "narrow"), axis=0, tiled=True),
-        lax.all_gather(memory_project, ("wide", "narrow"), axis=0, tiled=True),
-        lax.all_gather(cross_output, ("wide", "narrow"), axis=0, tiled=True),
-        lax.all_gather(expand_weight, ("wide", "narrow"), axis=0, tiled=True),
-        lax.all_gather(contract_weight, ("wide", "narrow"), axis=0, tiled=True),
-        lax.all_gather(norm_gain, ("wide", "narrow"), axis=1, tiled=True),
-        lax.all_gather(norm_bias, ("wide", "narrow"), axis=1, tiled=True),
-    )
+    rows, width = cross_output.shape
+    folds = contract_weight.shape[0] // rows
+    folded = contract_weight.reshape(folds, rows, width).transpose(1, 0, 2).reshape(rows, -1)
+    norms = jnp.concatenate([norm_gain, norm_bias], axis=0).T
+    packed = jnp.concatenate(
+        [
+            self_project,
+            self_output,
+            cross_project,
+            memory_project,
+            cross_output,
+            expand_weight,
+            folded,
+            jnp.pad(norms, ((0, 0), (0, 128 - norms.shape[1]))),
+        ],
+        axis=1,
+    )
+    whole = gather_shards(packed)
+    out = []
+    start = 0
+    for part in (self_project, self_output, cross_project, memory_project, cross_output, expand_weight):
+        out.append(whole[:, :, start : start + part.shape[1]].reshape(-1, part.shape[1]))
+        start += part.shape[1]
+    span = folded.shape[1]
+    contract = whole[:, :, start : start + span].reshape(-1, rows, folds, width)
+    out.append(contract.transpose(0, 2, 1, 3).reshape(-1, width))
+    start += span
+    count = norm_gain.shape[0]
+    out.append(whole[:, :, start : start + count].reshape(-1, count).T)
+    out.append(whole[:, :, start + count : start + 2 * count].reshape(-1, count).T)
+    return tuple(out)
 
 
 def settle_grads(
@@ -122,17 +230,34 @@
     gain_grad,
     offset_grad,
 ):
-    return (
-        lax.psum_scatter(project_grad, ("wide", "narrow"), scatter_dimension=0, tiled=True),
-        lax.psum_scatter(output_grad, ("wide", "narrow"), scatter_dimension=0, tiled=True),
-        lax.psum_scatter(cross_grad, ("wide", "narrow"), scatter_dimension=0, tiled=True),
-        lax.psum_scatter(memory_proj_grad, ("wide", "narrow"), scatter_dimension=0, tiled=True),
-        lax.psum_scatter(cross_out_grad, ("wide", "narrow"), scatter_dimension=0, tiled=True),
-        lax.psum_scatter(expand_grad, ("wide", "narrow"), scatter_dimension=0, tiled=True),
-        lax.psum_scatter(contract_grad, ("wide", "narrow"), scatter_dimension=0, tiled=True),
-        lax.psum_scatter(gain_grad, ("wide", "narrow"), scatter_dimension=1, tiled=True),
-        lax.psum_scatter(offset_grad, ("wide", "narrow"), scatter_dimension=1, tiled=True),
-    )
+    device_count = lax.axis_size("wide") * lax.axis_size("narrow")
+    straight = (project_grad, output_grad, cross_grad, memory_proj_grad, cross_out_grad, expand_grad)
+    width = output_grad.shape[1]
+    rows = output_grad.shape[0] // device_count
+    folds = contract_grad.shape[0] // output_grad.shape[0]
+    folded = contract_grad.reshape(device_count, folds, rows, width).transpose(0, 2, 1, 3)
+    folded = folded.reshape(device_count, rows, folds * width)
+    norms = jnp.concatenate([gain_grad, offset_grad], axis=0).T
+    norms = jnp.pad(norms, ((0, 0), (0, 128 - norms.shape[1])))
+    terms = jnp.concatenate(
+        [part.reshape(device_count, rows, -1) for part in straight]
+        + [folded, norms.reshape(device_count, rows, 128)],
+        axis=2,
+    )
+    own = scatter_sums(terms)
+    out = []
+    start = 0
+    for part in straight:
+        out.append(own[:, start : start + part.shape[1]])
+        start += part.shape[1]
+    span = folds * width
+    contract = own[:, start : start + span].reshape(rows, folds, width).transpose(1, 0, 2)
+    out.append(contract.reshape(folds * rows, width))
+    start += span
+    count = gain_grad.shape[0]
+    out.append(own[:, start : start + count].T)
+    out.append(own[:, start + count : start + 2 * count].T)
+    return tuple(out)
 
 
 def per_device(
@@ -234,27 +359,6 @@
         gain_rows[2],
         offset_rows[2],
     )
-    (
-        self_whole,
-        sout_whole,
-        cproj_whole,
-        mproj_whole,
-        cout_whole,
-        expand_whole,
-        contract_whole,
-        gain_whole,
-        offset_whole,
-    ) = fetch_weights(
-        self_project,
-        self_output,
-        cross_project,
-        memory_project,
-        cross_output,
-        expand_weight,
-        contract_weight,
-        norm_gain,
-        norm_bias,
-    )
     third_grad, gain_three, offset_three = third_pull(out_grad)
     ffn_grad = third_grad.astype(jnp.bfloat16)
     hidden = jnp.dot(second_low, expand_whole, preferred_element_type=jnp.float32)

time: 1930 us -> 708 us (0.37)
  waiting for transfers between devices: 1290 us -> 201 us
  blocking collectives: 200 us -> 0 us
  local copies, waits for them, and re-layouts: 71 us -> 142 us
  matrix products: 307 us -> 278 us
    reduce_scatter x5 -> x0, waiting for transfers between devices: 669 us -> none  [the longest x1 140 us: settle_grads(): lax.psum_scatter(contract_grad, ('wide', 'narrow'), scatter_dimension=0,...]
    unnamed x21 -> x4, waiting for transfers between devices: 499 us -> 0.07 us
    all_gather x5 -> x0, blocking collectives: 200 us -> none  [the longest x1 42.7 us: fetch_weights(): lax.all_gather(cross_output, ('wide', 'narrow'), axis=0, tiled=True)]
    ppermute x0 -> x14, waiting for transfers between devices: none -> 125 us  [exchange(): return lax.ppermute(block, ('wide', 'narrow'), pairs)]
    all_gather x4 -> x0, waiting for transfers between devices: 112 us -> none  [the longest x1 58.5 us: fetch_weights(): lax.all_gather(memory_project, ('wide', 'narrow'), axis=0, tiled=True)]
    reduce_scatter x1, waiting for transfers between devices: 0.02 us -> 42.5 us  [per_device(): lax.psum_scatter(memory_terms.astype(jnp.bfloat16), 'narrow', scatter_dim...]
    concatenate x0 -> x10, local copies, waits for them, and re-layouts: none -> 22.6 us  [the longest x2 7.87 us: per_device(): jnp.concatenate([merge_heads(cross_key_grad), merge_heads(cross_value_gra...]
    all_gather x1, waiting for transfers between devices: 0.01 us -> 20.1 us  [per_device(): pair_rows = lax.all_gather(pair_low, 'narrow', axis=1, tiled=True)]
  transfers between devices with their start and end apart: 17 -> 18, of which waited for: 12 -> 13; matrix products, arithmetic and copies ran while one was open for 15% -> 19% of each run, Pallas kernels for 0% -> 0%
where the time goes in v1:
time: 708 us; the launch traced here: 694 us
  matrix products  278 us (39%)
  waiting for transfers between devices  201 us (28%)
  local copies, waits for them, and re-layouts  142 us (20%)
  other arithmetic  40.4 us (6%)
  starting transfers between devices  17.8 us (3%)
  between operations  14.6 us (2%)
    ppermute x14, waiting for transfers between devices, exchange(): return lax.ppermute(block, ('wide', 'narrow'), pairs)  125 us
    dot_general x32, matrix products, one_head(): jnp.einsum('rqd,rkd->rqk', query_head, key_head, preferred_element_type=j...  71.9 us
    reduce_scatter x1, waiting for transfers between devices, per_device(): lax.psum_scatter(memory_terms.astype(jnp.bfloat16), 'narrow', scatter_dim...  42.5 us
    dot_general x16, matrix products, one_head(): jnp.einsum('rqk,rkd->rqd', score_grad, key_head, preferred_element_type=j...  39.1 us
    dot_general x16, matrix products, one_head(): jnp.einsum('rqk,rkd->rqd', prob_low, value_head, preferred_element_type=j...  38.7 us
    dot_general x16, matrix products, one_head(): jnp.einsum('rqd,rkd->rqk', grad_head, value_head, preferred_element_type=...  28.5 us
    dot_general x16, matrix products, one_head(): jnp.einsum('rqk,rqd->rkd', score_grad, query_head, preferred_element_type...  27.1 us
    dot_general x16, matrix products, one_head(): jnp.einsum('rqk,rqd->rkd', probs_full.astype(jnp.bfloat16), grad_head, pr...  27 us
  transfers between devices with their start and end apart: 18, of which 13 were waited for; matrix products, arithmetic and copies ran while one was open for 19% of the time, Pallas kernels for 0%

profile of v1, /device:TPU:0, one launch (start us, length us, event | category | flops | bytes accessed | tf_op | source)
XLA Modules:
  0.0 694.3 jit_solution(1359967805246936010)
XLA Ops:
  13.5 3.1 collective-permute-start
  16.5 2.6 collective-permute-start.1
  19.3 8.6 %collective-permute-done = bf16[1,16,8320]{2,1,0:T(8,128)(2,1)S(1)} collective-permute-done((bf16[1,16,8320]{2,1,0:T(8,128)(2,1)S(1)}, bf16[1,16,8320]{2,1,0:T(8,128)(2,1)S(1)}, u32[]{:S(2)}, u32[]{:S(2)}) %collective-permute-start) | collective-permute-done | bytes 266272 | tf_op jit(solution)/shard_map/ppermute | solution.py:99
  27.9 10.3 %collective-permute-done.1 = bf16[1,16,8320]{2,1,0:T(8,128)(2,1)S(1)} collective-permute-done((bf16[1,16,8320]{2,1,0:T(8,128)(2,1)S(1)}, bf16[1,16,8320]{2,1,0:T(8,128)(2,1)S(1)}, u32[]{:S(2)}, u32[]{:S(2)}) %collective-permute-start.1) | collective-permute-done | bytes 266272 | tf_op jit(solution)/shard_map/ppermute | solution.py:99
  45.1 19.7 %collective-permute-done.3 = bf16[4,1,16,8320]{3,2,0,1:T(8,128)(2,1)S(1)} collective-permute-done((bf16[4,1,16,8320]{3,2,0,1:T(8,128)(2,1)S(1)}, bf16[4,1,16,8320]{3,2,0,1:T(8,128)(2,1)S(1)}, u32[]{:S(2)}, u32[]{:S(2)}) %collective-permute-start.3) | collective-permute-done | bytes 1064992 | tf_op jit(solution)/shard_map/ppermute | solution.py:99
  65.8 19.3 %collective-permute-done.4 = bf16[4,1,16,8320]{3,2,0,1:T(8,128)(2,1)S(1)} collective-permute-done((bf16[4,1,16,8320]{3,2,0,1:T(8,128)(2,1)S(1)}, bf16[4,1,16,8320]{3,2,0,1:T(8,128)(2,1)S(1)}, u32[]{:S(2)}, u32[]{:S(2)}) %collective-permute-start.4) | collective-permute-done | bytes 1064992 | tf_op jit(solution)/shard_map/ppermute | solution.py:99
  87.8 2.8 bitcast_dynamic-update-slice_fusion
  90.6 4.2 collective-permute-done.6
  94.8 2.8 bitcast_dynamic-update-slice_fusion.1
  97.6 3.2 copy-done
  111.8 4.2 fusion.163
  122.3 20.1 %all-gather.5.cloned.1.call-done = bf16[2048,1024]{0,1:T(8,128)(2,1)} async-done(((bf16[512,1024]{0,1:T(8,128)(2,1)}), bf16[2048,1024]{0,1:T(8,128)(2,1)}) %all-gather.5.cloned.1.call-update) | async-done | bytes 4194320 | tf_op jit(solution)/shard_map/all_gather | solution.py:317
  142.5 4.8 fusion.165
  147.2 4.8 copy.195
  152.1 4.8 copy.196
  156.9 38.1 %while.56 = (s32[]{:T(128)}, bf16[8,1,512,64]{2,3,1,0:T(8,128)(2,1)S(1)}, f32[8,1,512]{2,1,0:T(1,128)S(1)}, bf16[8,1,512,64]{3,2,1,0:T(8,128)(2,1)S(1)}, bf16[8,...) while((s32[]{:T(128)}, ...), condition=%wide.region_5.6_spmd.clone, body=%wide.region_2.0_spmd.clone.sunk | while | flops 277872128 | bytes 13926497 | solution.py:55
  201.0 4.8 fusion.164
  205.9 4.8 copy.201
  210.7 4.8 copy.202
  216.4 43.1 %while.57 = (s32[]{:T(128)}, bf16[8,1,512,64]{2,3,1,0:T(8,128)(2,1)}, f32[8,1,512]{2,1,0:T(1,128)S(1)}, bf16[8,1,512,64]{3,2,1,0:T(8,128)(2,1)S(1)}, bf16[8,1,20...) while((s32[]{:T(128)}, ...), condition=%wide.region_13.14_spmd.clone, body=%wide.region_10.13_spmd.clone.sunk | while | flops 277872128 | bytes 13926497 | solution.py:55
  219.0 2.7 fusion.239
  224.4 2.7 fusion.239
  229.8 2.7 fusion.239
  235.1 2.7 fusion.239
  240.5 2.7 fusion.239
  245.8 2.7 fusion.239
  251.2 2.7 fusion.239
  256.6 2.7 fusion.239
  261.8 3.5 fusion.95
  269.4 3.7 fusion.87
  282.8 86.7 %while.58 = (s32[]{:T(128)}, bf16[8,1,512,64]{2,3,1,0:T(8,128)(2,1)}, bf16[8,1,2048,64]{2,3,1,0:T(8,128)(2,1)}, bf16[8,1,2048,64]{2,3,1,0:T(8,128)(2,1)}, bf16[8...) while((s32[]{:T(128)}, ...), condition=%wide.region_24.25_spmd.clone, body=%wide.region_22.24_spmd.clone.sunk | while | flops 682622464 | bytes 34759800 | solution.py:87
  285.0 2.6 multiply_reduce_fusion.13
  328.2 2.6 multiply_reduce_fusion.13
  338.9 2.6 multiply_reduce_fusion.13
  378.7 86.2 %while.59 = (s32[]{:T(128)}, bf16[8,1,512,64]{2,3,1,0:T(8,128)(2,1)}, bf16[8,1,2048,64]{2,3,1,0:T(8,128)(2,1)}, bf16[8,1,2048,64]{2,3,1,0:T(8,128)(2,1)}, bf16[8...) while((s32[]{:T(128)}, ...), condition=%wide.region_29.30_spmd.clone, body=%wide.region_27.29_spmd.clone.sunk | while | flops 682622464 | bytes 34759800 | solution.py:87
  380.4 2.6 multiply_reduce_fusion.14
  391.2 2.6 multiply_reduce_fusion.14
  402.0 2.6 multiply_reduce_fusion.14
  412.8 2.6 multiply_reduce_fusion.14
  423.6 2.6 multiply_reduce_fusion.14
  434.3 2.6 multiply_reduce_fusion.14
  445.1 2.6 multiply_reduce_fusion.14
  455.9 2.6 multiply_reduce_fusion.14
  464.9 3.9 copy.212
  468.8 4.0 copy.213
  472.8 4.7 pad_maximum_fusion
  477.6 3.9 copy.216
  481.5 3.9 copy.217
  485.4 5.6 pad_maximum_fusion.1
  493.6 3.9 copy.223
  497.5 2.9 convert_bitcast_fusion
  500.4 3.3 copy.225
  503.7 4.6 concatenate.69
  509.4 13.0 %reduce-scatter.3.cloned.1.call-done = bf16[1,512,1024]{2,1,0:T(8,128)(2,1)} async-done(((bf16[1,2048,1024]{2,1,0:T(8,128)(2,1)}), bf16[1,512,1024]{2,1,0:T(8,128)(2,1)}) %reduce-scatter.3.cloned.1.call-update) | async-done | bytes 1048592 | tf_op jit(solution)/shard_map/reduce_scatter | solution.py:413
  527.0 42.5 %reduce-scatter.5.cloned.1.call-done = bf16[1,512,1024]{2,1,0:T(8,128)(2,1)} async-done(((bf16[1,2048,1024]{2,1,0:T(8,128)(2,1)}), bf16[1,512,1024]{2,1,0:T(8,128)(2,1)}) %reduce-scatter.5.cloned.1.call-update) | async-done | bytes 1048592 | tf_op jit(solution)/shard_map/reduce_scatter | solution.py:388
  578.3 2.6 fusion.96
  583.1 7.4 %copy.230 = bf16[2,2,2,2,2,16,8320]{6,5,4,3,2,1,0:T(8,128)(2,1)} copy(bf16[2,2,2,2,2,16,8320]{6,5,0,2,1,4,3:T(8,128)(2,1)} %bitcast.136) | data formatting | bytes 17039360 | tf_op jit(solution)/shard_map/transpose | solution.py:165
  590.5 2.6 dynamic-slice_bitcast_fusion
  593.2 7.2 %collective-permute-done.7 = bf16[16,16,8320]{2,1,0:T(8,128)(2,1)S(1)} collective-permute-done((bf16[16,16,8320]{2,1,0:T(8,128)(2,1)S(1)}, bf16[16,16,8320]{2,1,0:T(8,128)(2,1)S(1)}, u32[]{:S(2)}, u32[]{:S(2)}) %collective-permute-start.7) | collective-permute-done | bytes 4259872 | tf_op jit(solution)/shard_map/ppermute | solution.py:99
  610.0 22.8 %collective-permute-done.10 = bf16[4,16,8320]{2,1,0:T(8,128)(2,1)} collective-permute-done((bf16[4,16,8320]{2,1,0:T(8,128)(2,1)}, bf16[4,16,8320]{2,1,0:T(8,128)(2,1)}, u32[]{:S(2)}, u32[]{:S(2)}) %collective-permute-start.10) | collective-permute-done | bytes 1064992 | tf_op jit(solution)/shard_map/ppermute | solution.py:99
  632.8 22.0 %collective-permute-done.8 = bf16[4,16,8320]{2,1,0:T(8,128)(2,1)} collective-permute-done((bf16[4,16,8320]{2,1,0:T(8,128)(2,1)}, bf16[4,16,8320]{2,1,0:T(8,128)(2,1)}, u32[]{:S(2)}, u32[]{:S(2)}) %collective-permute-start.8) | collective-permute-done | bytes 1064992 | tf_op jit(solution)/shard_map/ppermute | solution.py:99
  654.9 2.7 fusion.100
  667.2 3.3 convolution_bitcast_fusion.7
  672.0 9.6 %collective-permute-done.12 = bf16[1,16,8320]{2,1,0:T(8,128)(2,1)} collective-permute-done((bf16[1,16,8320]{2,1,0:T(8,128)(2,1)S(1)}, bf16[1,16,8320]{2,1,0:T(8,128)(2,1)}, u32[]{:S(2)}, u32[]{:S(2)}) %collective-permute-start.12) | collective-permute-done | bytes 266272 | tf_op jit(solution)/shard_map/ppermute | solution.py:99
  (394 shorter events, 314.4 us)
Async XLA Ops:
  7.2 135.3 %all-gather.5.cloned.1.call-start = ((), (), s32[]{:S(2)}) async-start(), calls=%async_computation.4 | async-start | bytes 5242880 | tf_op jit(solution)/shard_map/all_gather | solution.py:317
  13.5 14.4 %collective-permute-start = (bf16[1,16,8320]{2,1,0:T(8,128)(2,1)S(1)}, bf16[1,16,8320]{2,1,0:T(8,128)(2,1)S(1)}, u32[]{:S(2)}, u32[]{:S(2)}) collective-permute-start(bf16[1,16,8320]{2,1,0:T(8,128)(2,1)S(1)} %bitcast.560), channel_id=1, source_target_pairs={{0,8},{1,9},{2,10},{3,11},{4,12},{5,13},{6,14},{7,15},{8,0},{9,1},... | collective-permute-start | bytes 798728 | tf_op jit(solution)/shard_map/ppermute | solution.py:99
  16.5 21.6 %collective-permute-start.1 = (bf16[1,16,8320]{2,1,0:T(8,128)(2,1)S(1)}, bf16[1,16,8320]{2,1,0:T(8,128)(2,1)S(1)}, u32[]{:S(2)}, u32[]{:S(2)}) collective-permute-start(bf16[1,16,8320]{2,1,0:T(8,128)(2,1)S(1)} %bitcast.561), channel_id=1, source_target_pairs={{0,16},{1,17},{2,18},{3,19},{4,20},{5,21},{6,22},{7,23},{8,24},{9,... | collective-permute-start | bytes 798728 | tf_op jit(solution)/shard_map/ppermute | solution.py:99
  19.1 19.1 %collective-permute-start.2 = (bf16[1,16,8320]{2,1,0:T(8,128)(2,1)S(1)}, bf16[1,16,8320]{2,1,0:T(8,128)(2,1)S(1)}, u32[]{:S(2)}, u32[]{:S(2)}) collective-permute-start(bf16[1,16,8320]{2,1,0:T(8,128)(2,1)S(1)} %bitcast.562), channel_id=1, source_target_pairs={{0,24},{1,25},{2,26},{3,27},{4,28},{5,29},{6,30},{7,31},{8,16},{9,... | collective-permute-start | bytes 798728 | tf_op jit(solution)/shard_map/ppermute | solution.py:99
  38.3 26.5 %collective-permute-start.3 = (bf16[4,1,16,8320]{3,2,0,1:T(8,128)(2,1)S(1)}, bf16[4,1,16,8320]{3,2,0,1:T(8,128)(2,1)S(1)}, u32[]{:S(2)}, u32[]{:S(2)}) collective-permute-start(bf16[4,1,16,8320]{3,2,0,1:T(8,128)(2,1)S(1)} %bitcast_dynamic-update-slice_fusion.6), channel_id=1, source_target_pairs={{0,2},{1,3},{2,0},{3,1},{4,6},{5,7},{6,4},{7,5},{8,10},{9,11},{10,... | collective-permute-start | bytes 3194888 | tf_op jit(solution)/shard_map/ppermute | solution.py:99
  39.8 45.3 %collective-permute-start.4 = (bf16[4,1,16,8320]{3,2,0,1:T(8,128)(2,1)S(1)}, bf16[4,1,16,8320]{3,2,0,1:T(8,128)(2,1)S(1)}, u32[]{:S(2)}, u32[]{:S(2)}) collective-permute-start(bf16[4,1,16,8320]{3,2,0,1:T(8,128)(2,1)S(1)} %bitcast_dynamic-update-slice_fusion.6), channel_id=1, source_target_pairs={{0,4},{1,5},{2,6},{3,7},{4,0},{5,1},{6,2},{7,3},{8,12},{9,13},{10,... | collective-permute-start | bytes 3194888 | tf_op jit(solution)/shard_map/ppermute | solution.py:99
  41.3 44.8 %collective-permute-start.5 = (bf16[4,1,16,8320]{3,2,0,1:T(8,128)(2,1)S(1)}, bf16[4,1,16,8320]{3,2,0,1:T(8,128)(2,1)S(1)}, u32[]{:S(2)}, u32[]{:S(2)}) collective-permute-start(bf16[4,1,16,8320]{3,2,0,1:T(8,128)(2,1)S(1)} %bitcast_dynamic-update-slice_fusion.6), channel_id=1, source_target_pairs={{0,6},{1,7},{2,4},{3,5},{4,2},{5,3},{6,0},{7,1},{8,14},{9,15},{10,... | collective-permute-start | bytes 3194888 | tf_op jit(solution)/shard_map/ppermute | solution.py:99
  87.2 7.6 %collective-permute-start.6 = (bf16[4,4,1,16,8320]{4,3,0,1,2:T(8,128)(2,1)}, bf16[4,4,1,16,8320]{4,3,0,1,2:T(8,128)(2,1)}, u32[]{:S(2)}, u32[]{:S(2)}) collective-permute-start(bf16[4,4,1,16,8320]{4,3,0,1,2:T(8,128)(2,1)} %bitcast_dynamic-update-slice_fusion.5), channel_id=1, source_target_pairs={{0,1},{1,0},{2,3},{3,2},{4,5},{5,4},{6,7},{7,6},{8,9},{9,8},{10,11... | collective-permute-start | bytes 12779528 | tf_op jit(solution)/shard_map/ppermute | solution.py:99
  90.6 11.6 %copy-start.27 = (bf16[1,512,512]{2,1,0:T(8,128)(2,1)S(1)}, bf16[1,512,512]{2,1,0:T(8,128)(2,1)}, u32[]{:S(2)}) copy-start(bf16[1,512,512]{2,1,0:T(8,128)(2,1)} %param.22) | copy-start | bytes 1572868
  97.6 3.3 copy-start
  100.8 4.2 copy-start.32
  100.8 4.4 copy-start.33
  100.8 4.6 copy-start.11
  101.0 1.1 copy-start.20
  103.9 97.1 %all-gather.7.cloned.1.call-start = ((), (), s32[]{:S(2)}) async-start(), calls=%async_computation.5 | async-start | bytes 5242880 | tf_op jit(solution)/shard_map/all_gather | solution.py:339
  115.9 4.1 copy-start.24
  115.9 4.1 copy-start.28
  120.0 78.1 %copy-start.5 = (bf16[32,16,512]{2,1,0:T(8,128)(2,1)}, bf16[32,16,512]{2,1,0:T(8,128)(2,1)S(1)}, u32[]{:S(2)}) copy-start(bf16[32,16,512]{2,1,0:T(8,128)(2,1)S(1)} %get-tuple-element.445) | copy-start | bytes 1572868
  121.8 400.6 %reduce-scatter.3.cloned.1.call-start = ((), (), s32[]{:S(2)}) async-start(), calls=%async_computation.2 | async-start | bytes 5242880 | tf_op jit(solution)/shard_map/reduce_scatter | solution.py:413
  195.1 1.0 copy-start.4
  195.1 4.4 copy-start.6
  198.2 1.3 copy-start.13
  259.5 2.3 copy-start.19
  261.8 3.6 copy-start.25
  261.8 3.5 copy-start.16
  269.4 3.8 copy-start.22
  273.1 1.8 copy-start.34
  273.1 2.1 copy-start.9
  369.5 2.4 copy-start.8
  477.5 92.0 %reduce-scatter.5.cloned.1.call-start = ((), (), s32[]{:S(2)}) async-start(), calls=%async_computation.3 | async-start | bytes 5242880 | tf_op jit(solution)/shard_map/reduce_scatter | solution.py:388
  491.0 2.2 copy-start.12
  493.3 4.3 copy-start.23
  500.4 7.9 %copy-start.17 = (bf16[8,1,512,64]{2,3,1,0:T(8,128)(2,1)S(1)}, bf16[8,1,512,64]{2,3,1,0:T(8,128)(2,1)}, u32[]{:S(2)}) copy-start(bf16[8,1,512,64]{2,3,1,0:T(8,128)(2,1)} %get-tuple-element.201) | copy-start | bytes 1572868
  500.4 22.0 %copy-start.18 = (bf16[1,512,512]{1,2,0:T(8,128)(2,1)S(1)}, bf16[1,512,512]{1,2,0:T(8,128)(2,1)}, u32[]{:S(2)}) copy-start(bf16[1,512,512]{1,2,0:T(8,128)(2,1)} %copy.182) | copy-start | bytes 1572868
  524.8 44.7 %copy-start.30 = (bf16[1,512,512]{1,2,0:T(8,128)(2,1)S(1)}, bf16[1,512,512]{1,2,0:T(8,128)(2,1)}, u32[]{:S(2)}) copy-start(bf16[1,512,512]{1,2,0:T(8,128)(2,1)} %copy.200) | copy-start | bytes 1572868
  569.5 2.7 copy-start.7
  569.5 4.1 copy-start.14
  569.5 4.1 copy-start.15
  572.2 6.1 copy-start.26
  572.2 6.1 copy-start.35
  578.3 2.6 copy-start.3
  590.5 10.0 %copy-start.1 = (bf16[2,2,2,2,2,16,8320]{6,5,4,3,2,1,0:T(8,128)(2,1)S(1)}, bf16[2,2,2,2,2,16,8320]{6,5,4,3,2,1,0:T(8,128)(2,1)}, u32[]{:S(2)}) copy-start(bf16[2,2,2,2,2,16,8320]{6,5,4,3,2,1,0:T(8,128)(2,1)} %copy.230) | copy-start | bytes 25559044
  593.2 7.3 %collective-permute-start.7 = (bf16[16,16,8320]{2,1,0:T(8,128)(2,1)S(1)}, bf16[16,16,8320]{2,1,0:T(8,128)(2,1)S(1)}, u32[]{:S(2)}, u32[]{:S(2)}) collective-permute-start(bf16[16,16,8320]{2,1,0:T(8,128)(2,1)S(1)} %dynamic-slice_bitcast_fusion), channel_id=1, source_target_pairs={{0,1},{1,0},{2,3},{3,2},{4,5},{5,4},{6,7},{7,6},{8,9},{9,8},{10,11... | collective-permute-start | bytes 12779528 | tf_op jit(solution)/shard_map/ppermute | solution.py:99
  601.5 2.0 copy-start.2
  601.5 7.2 %copy-start.10 = (f32[1,512,512]{1,2,0:T(8,128)S(1)}, f32[1,512,512]{1,2,0:T(8,128)}, u32[]{:S(2)}) copy-start(f32[1,512,512]{1,2,0:T(8,128)} %get-tuple-element.461) | copy-start | bytes 3145732
  605.2 27.6 %collective-permute-start.10 = (bf16[4,16,8320]{2,1,0:T(8,128)(2,1)}, bf16[4,16,8320]{2,1,0:T(8,128)(2,1)}, u32[]{:S(2)}, u32[]{:S(2)}) collective-permute-start(bf16[4,16,8320]{2,1,0:T(8,128)(2,1)} %get-tuple-element.452), channel_id=1, source_target_pairs={{0,6},{1,7},{2,4},{3,5},{4,2},{5,3},{6,0},{7,1},{8,14},{9,15},{10,... | collective-permute-start | bytes 3194888 | tf_op jit(solution)/shard_map/ppermute | solution.py:99
  606.7 48.2 %collective-permute-start.8 = (bf16[4,16,8320]{2,1,0:T(8,128)(2,1)}, bf16[4,16,8320]{2,1,0:T(8,128)(2,1)}, u32[]{:S(2)}, u32[]{:S(2)}) collective-permute-start(bf16[4,16,8320]{2,1,0:T(8,128)(2,1)} %get-tuple-element.451), channel_id=1, source_target_pairs={{0,2},{1,3},{2,0},{3,1},{4,6},{5,7},{6,4},{7,5},{8,10},{9,11},{10,... | collective-permute-start | bytes 3194888 | tf_op jit(solution)/shard_map/ppermute | solution.py:99
  608.1 46.7 %collective-permute-start.9 = (bf16[4,16,8320]{2,1,0:T(8,128)(2,1)}, bf16[4,16,8320]{2,1,0:T(8,128)(2,1)}, u32[]{:S(2)}, u32[]{:S(2)}) collective-permute-start(bf16[4,16,8320]{2,1,0:T(8,128)(2,1)} %get-tuple-element.453), channel_id=1, source_target_pairs={{0,4},{1,5},{2,6},{3,7},{4,0},{5,1},{6,2},{7,3},{8,12},{9,13},{10,... | collective-permute-start | bytes 3194888 | tf_op jit(solution)/shard_map/ppermute | solution.py:99
  608.7 54.0 %copy-start.29 = (bf16[1,512,512]{2,1,0:T(8,128)(2,1)S(1)}, bf16[1,512,512]{2,1,0:T(8,128)(2,1)}, u32[]{:S(2)}) copy-start(bf16[1,512,512]{2,1,0:T(8,128)(2,1)} %copy.214) | copy-start | bytes 1572868
  610.0 52.7 %copy-start.21 = (bf16[32,16,1536]{2,1,0:T(8,128)(2,1)S(1)}, bf16[32,16,1536]{2,1,0:T(8,128)(2,1)}, u32[]{:S(2)}) copy-start(bf16[32,16,1536]{2,1,0:T(8,128)(2,1)} %copy-done.20) | copy-start | bytes 4718596
  610.0 52.7 %copy-start.31 = (bf16[1,512,1024]{2,1,0:T(8,128)(2,1)S(1)}, bf16[1,512,1024]{2,1,0:T(8,128)(2,1)}, u32[]{:S(2)}) copy-start(bf16[1,512,1024]{2,1,0:T(8,128)(2,1)} %reduce-scatter.3.cloned.1.call-done) | copy-start | bytes 3145732
  658.3 13.6 %collective-permute-start.11 = (bf16[1,16,8320]{2,1,0:T(8,128)(2,1)}, bf16[1,16,8320]{2,1,0:T(8,128)(2,1)}, u32[]{:S(2)}, u32[]{:S(2)}) collective-permute-start(bf16[1,16,8320]{2,1,0:T(8,128)(2,1)} %get-tuple-element.458), channel_id=1, source_target_pairs={{0,8},{1,9},{2,10},{3,11},{4,12},{5,13},{6,14},{7,15},{8,0},{9,1},... | collective-permute-start | bytes 798728 | tf_op jit(solution)/shard_map/ppermute | solution.py:99
  659.8 21.7 %collective-permute-start.12 = (bf16[1,16,8320]{2,1,0:T(8,128)(2,1)S(1)}, bf16[1,16,8320]{2,1,0:T(8,128)(2,1)}, u32[]{:S(2)}, u32[]{:S(2)}) collective-permute-start(bf16[1,16,8320]{2,1,0:T(8,128)(2,1)S(1)} %get-tuple-element.460), channel_id=1, source_target_pairs={{0,16},{1,17},{2,18},{3,19},{4,20},{5,21},{6,22},{7,23},{8,24},{9,... | collective-permute-start | bytes 798728 | tf_op jit(solution)/shard_map/ppermute | solution.py:99
  662.2 19.3 %collective-permute-start.13 = (bf16[1,16,8320]{2,1,0:T(8,128)(2,1)S(1)}, bf16[1,16,8320]{2,1,0:T(8,128)(2,1)}, u32[]{:S(2)}, u32[]{:S(2)}) collective-permute-start(bf16[1,16,8320]{2,1,0:T(8,128)(2,1)S(1)} %get-tuple-element.459), channel_id=1, source_target_pairs={{0,24},{1,25},{2,26},{3,27},{4,28},{5,29},{6,30},{7,31},{8,16},{9,... | collective-permute-start | bytes 798728 | tf_op jit(solution)/shard_map/ppermute | solution.py:99
Sparse Core Ops, SparseCore 0:
  104.0 38.3 all-gather.4
  144.6 34.4 all-gather.6
  477.6 44.7 reduce-scatter.2
  524.9 44.4 reduce-scatter.4

commit v2 on v0

v2 whole, which is shorter than its diff:
```python
import functools

import jax
import jax.numpy as jnp
from jax import lax
from jax.experimental import pallas as pl
from jax.experimental.pallas import tpu as pltpu
from jax.sharding import PartitionSpec as P

HEAD_DIM = 64
LANES = 128
TILE_ROWS = 16
BLOCKS = 32
AXES = ("wide", "narrow")
LOW = jnp.bfloat16
FULL = jnp.float32

ln_eps = 1e-05
score_scale = HEAD_DIM ** (-0.5)
mask_step = -(2.0**30)

BY_LANES = (((1,), (1,)), ((), ()))
PLAIN = (((1,), (0,)), ((), ()))
VMEM_BYTES = 58 * 2**20


def dot(left, right, dims=PLAIN):
    return lax.dot_general(left, right, dims, preferred_element_type=FULL)


def exchange(block, mask):
    device_count = lax.axis_size("wide") * lax.axis_size("narrow")
    pairs = [(device, device ^ mask) for device in range(device_count)]
    return lax.ppermute(block, AXES, pairs)


def device_number():
    return lax.axis_index("wide") * lax.axis_size("narrow") + lax.axis_index("narrow")


def staged():
    return lax.axis_size("wide") * lax.axis_size("narrow") == BLOCKS


FAR = (8, 16, 24)
PLANE = (2, 4, 6)


def gather_far(shard):
    if not staged():
        return shard
    return jnp.stack([shard] + [exchange(shard, mask) for mask in FAR])


def gather_plane(held):
    if not staged():
        return held
    return [held] + [exchange(held, mask) for mask in PLANE]


def gather_core(held, folds=0):
    if staged():
        return held + [exchange(quarter, 1) for quarter in held]
    whole = lax.all_gather(held, AXES, axis=0, tiled=True)
    if folds:
        rows, columns = held.shape
        split = columns - folds * whole.shape[0]
        tall = unfold_rows(held[:, split:], whole.shape[0])
        tall = lax.all_gather(tall, AXES, axis=0, tiled=True)
        tall = tall.reshape(BLOCKS, folds, TILE_ROWS, -1).transpose(0, 2, 1, 3)
        whole = jnp.concatenate([whole[:, :split], tall.reshape(whole.shape[0], -1)], axis=1)
    whole = whole.reshape(4, 4, 2, TILE_ROWS, held.shape[1]).transpose(2, 1, 0, 3, 4)
    return [whole[core, plane] for core in range(2) for plane in range(4)]


def home_number():
    return device_number() if staged() else jnp.zeros((), jnp.int32)


def block_number(home, core, plane, far):
    return home ^ (far * 8 + plane * 2 + core)


def reduce_core(kept, sent):
    if not staged():
        return kept, sent
    other = exchange(sent, 1)
    total = kept.astype(FULL) + other.astype(FULL)
    return total.astype(LOW)


def reduce_plane(held):
    if not staged():
        return held
    total = held[0].astype(FULL)
    for plane, mask in enumerate(PLANE):
        total = total + exchange(held[plane + 1], mask).astype(FULL)
    return total.astype(LOW)


def reduce_far(held, folds=0):
    if staged():
        total = held[0].astype(FULL)
        for far, mask in enumerate(FAR):
            total = total + exchange(held[far + 1], mask).astype(FULL)
        return total
    whole = jnp.stack(held).transpose(2, 1, 0, 3, 4)
    whole = whole.reshape(BLOCKS * TILE_ROWS, -1).astype(FULL)
    if folds:
        split = whole.shape[1] - folds * whole.shape[0]
        tall = whole[:, split:].reshape(BLOCKS, TILE_ROWS, folds, -1).transpose(0, 2, 1, 3)
        tall = tall.reshape(folds * whole.shape[0], -1)
        tall = lax.psum_scatter(tall, AXES, scatter_dimension=0, tiled=True)
        whole = lax.psum_scatter(whole[:, :split], AXES, scatter_dimension=0, tiled=True)
        return jnp.concatenate([whole, fold_rows(tall, whole.shape[0])], axis=1)
    return lax.psum_scatter(whole, AXES, scatter_dimension=0, tiled=True)


def fold_rows(block, rows):
    return jnp.concatenate(
        [block[at : at + rows] for at in range(0, block.shape[0], rows)], axis=1
    )


def unfold_rows(block, width):
    return jnp.concatenate(
        [block[:, at : at + width] for at in range(0, block.shape[1], width)], axis=0
    )


def lane_numbers(shape):
    return lax.broadcasted_iota(jnp.int32, shape, 1)


def segment_bounds(lengths_ref):
    lane = lane_numbers((1, LANES)) & (HEAD_DIM - 1)
    first = jnp.full((1, LANES), 2**30, jnp.int32)
    last = jnp.zeros((1, LANES), jnp.int32)
    start = jnp.int32(0)
    count = lengths_ref.shape[1]
    for segment in range(count + 1):
        end = start + lengths_ref[0, segment] if segment < count else jnp.int32(2**30)
        first = jnp.where(lane == segment, start, first)
        last = jnp.where(lane == segment, end, last)
        start = end
    return first, last


def segment_flags(start, rows, bounds):
    position = start + lax.broadcasted_iota(jnp.int32, (rows, LANES), 0)
    return (position >= bounds[0]) & (position < bounds[1])


def three_parts(value):
    first = value.astype(LOW)
    rest = value - first.astype(FULL)
    second = rest.astype(LOW)
    third = (rest - second.astype(FULL)).astype(LOW)
    return first.astype(FULL), second.astype(FULL), third.astype(FULL)


def with_parts(base, value, lane, slot):
    first, second, third = three_parts(value)
    base = jnp.where(lane == slot, first, base)
    base = jnp.where(lane == slot + 1, second, base)
    return jnp.where(lane == slot + 2, third, base)


def query_flags(lengths_ref, start, rows):
    segments = lengths_ref.shape[1] + 1
    lane = lane_numbers((rows, LANES)) & (HEAD_DIM - 1)
    own = segment_flags(start, rows, segment_bounds(lengths_ref))
    return jnp.where(own | (lane >= segments), 0.0, mask_step)


def key_flags(lengths_ref, start, rows):
    segments = lengths_ref.shape[1] + 1
    lane = lane_numbers((rows, LANES)) & (HEAD_DIM - 1)
    own = segment_flags(start, rows, segment_bounds(lengths_ref))
    return jnp.where(own | ((lane >= segments) & (lane < segments + 3)), 1.0, 0.0).astype(LOW)


def fill_weight(target, quarters, home, columns):
    first, folds = columns
    width = target.shape[1]
    for core in range(2):
        for plane in range(4):
            for far in range(4):
                block = block_number(home, core, plane, far)
                piece = quarters[core * 4 + plane]
                for fold in range(folds):
                    row = pl.multiple_of(block * (TILE_ROWS * folds) + fold * TILE_ROWS, TILE_ROWS)
                    start = first + fold * width
                    target[pl.ds(row, TILE_ROWS), :] = piece[far, :, start : start + width]


def pack_grad(source, kept, sent, home, columns):
    first, folds = columns
    width = source.shape[1]
    for core, target in ((0, kept), (1, sent)):
        for plane in range(4):
            for far in range(4):
                block = block_number(home, core, plane, far)
                for fold in range(folds):
                    row = pl.multiple_of(block * (TILE_ROWS * folds) + fold * TILE_ROWS, TILE_ROWS)
                    start = first + fold * width
                    target[plane, far, :, start : start + width] = source[pl.ds(row, TILE_ROWS), :]


def normalise(states):
    centred = states - jnp.mean(states, axis=1, keepdims=True)
    spread = jnp.mean(centred * centred, axis=1, keepdims=True)
    scale = lax.rsqrt(spread + ln_eps)
    return centred * scale, scale


def norm_backward(cotangent, unit, scale, gain):
    scaled = cotangent * gain
    grad = scale * (
        scaled
        - jnp.mean(scaled, axis=1, keepdims=True)
        - unit * jnp.mean(scaled * unit, axis=1, keepdims=True)
    )
    return (
        grad,
        jnp.sum(cotangent * unit, axis=0, keepdims=True),
        jnp.sum(cotangent, axis=0, keepdims=True),
    )


KEY_STEP = 256


def attend_pair(query, flags, key_aug, value_aug, segments):
    rows = query.shape[0]
    keys = key_aug.shape[1]
    lane = lane_numbers((rows, LANES))
    mixes = []
    kept = []
    for head in range(2):
        mine = (lane < HEAD_DIM) if head == 0 else (lane >= HEAD_DIM)
        slot = segments + (HEAD_DIM if head == 0 else 0)
        base = jnp.where(mine, query, flags)
        plain = base.astype(LOW)
        peak = jnp.full((rows, LANES), -jnp.inf, FULL)
        for start in range(0, keys, KEY_STEP):
            scores = dot(plain, key_aug[head, start : start + KEY_STEP], BY_LANES)
            for at in range(0, KEY_STEP, LANES):
                peak = jnp.maximum(peak, scores[:, at : at + LANES])
        peak = jnp.max(peak, axis=1, keepdims=True)
        shifted = with_parts(base, -peak, lane, slot).astype(LOW)
        total = jnp.zeros((rows, LANES), FULL)
        for start in range(0, keys, KEY_STEP):
            scores = dot(shifted, key_aug[head, start : start + KEY_STEP], BY_LANES)
            weights = jnp.exp(scores).astype(LOW)
            total = total + dot(weights, value_aug[head, start : start + KEY_STEP])
        weight_sum = total[:, HEAD_DIM : HEAD_DIM + 1] if head == 0 else total[:, 0:1]
        kept.append(with_parts(base, -(peak + jnp.log(weight_sum)), lane, slot).astype(LOW))
        mixes.append(total / weight_sum)
    return jnp.where(lane < HEAD_DIM, mixes[0], mixes[1]).astype(LOW), kept


def widen_pair(key, value, flags, key_aug, value_aug, start):
    rows = key.shape[0]
    lane = lane_numbers((rows, LANES))
    ones = jnp.ones((rows, LANES), LOW)
    for head in range(2):
        mine = (lane < HEAD_DIM) if head == 0 else (lane >= HEAD_DIM)
        key_aug[head, start : start + rows] = jnp.where(mine, key, flags)
        value_aug[head, start : start + rows] = jnp.where(mine, value, ones)


def pair_columns(first, pair):
    return pl.ds(pl.multiple_of(first + pair * LANES, LANES), LANES)


def self_forward_kernel(
    info, lengths, rows_0, rows_1, rows_2, rows_3, *refs
):
    quarters = refs[:8]
    mix_ref, query_ref, key_ref, value_ref, weight, flags_q, flags_k, key_aug, value_aug = refs[8:]
    pair = pl.program_id(0)
    home, place = info[0], info[1]
    local, width = rows_0.shape
    segments = lengths.shape[1] + 1

    @pl.when(pair == 0)
    def _():
        fill_weight(weight, quarters, home, (0, 1))
        flags_q[...] = query_flags(lengths, place * local, local)
        for step in range(4):
            flags_k[step * local : (step + 1) * local] = key_flags(
                lengths, (place ^ step) * local, local
            )

    both = jnp.concatenate(
        [weight[:, pair_columns(width, pair)], weight[:, pair_columns(2 * width, pair)]], axis=1
    )
    for step, rows in enumerate((rows_0, rows_1, rows_2, rows_3)):
        start = step * local
        made = dot(rows[...], both).astype(LOW)
        key, value = made[:, :LANES], made[:, LANES:]
        key_ref[start : start + local] = key
        value_ref[start : start + local] = value
        widen_pair(key, value, flags_k[start : start + local], key_aug, value_aug, start)
    query = dot(rows_0[...], weight[:, pair_columns(0, pair)]).astype(LOW).astype(FULL)
    mix, kept = attend_pair(query * score_scale, flags_q[...], key_aug, value_aug, segments)
    mix_ref[...] = mix
    query_ref[0] = kept[0]
    query_ref[1] = kept[1]


def cross_forward_kernel(
    info, target_lengths, source_lengths, mix, states, rows_0, rows_1, rows_2, rows_3, *refs
):
    quarters = refs[:8]
    (
        mix_ref,
        query_ref,
        key_ref,
        value_ref,
        unit_ref,
        scale_ref,
        norms_ref,
        out_weight,
        query_weight,
        pair_weight,
        norm_rows,
        queries,
        flags_q,
        flags_k,
        key_aug,
        value_aug,
    ) = refs[8:]
    pair = pl.program_id(0)
    home, place = info[0], info[1]
    local, width = rows_0.shape
    segments = target_lengths.shape[1] + 1

    @pl.when(pair == 0)
    def _():
        fill_weight(out_weight, quarters, home, (0, 1))
        fill_weight(query_weight, quarters, home, (width, 1))
        fill_weight(pair_weight, quarters, home, (2 * width, 1))
        fill_weight(norm_rows, quarters, home, (4 * width, 1))
        norms = norm_rows[...].astype(FULL).T[0:8]
        norms_ref[...] = norms
        mixed = states[...].astype(FULL) + dot(mix[...], out_weight[...])
        unit, scale = normalise(mixed)
        unit_ref[...] = unit
        scale_ref[...] = jnp.broadcast_to(scale, (local, LANES))
        first_low = (unit * norms[0:1] + norms[3:4]).astype(LOW)
        made = dot(first_low, query_weight[...]).astype(LOW)
        for at in range(queries.shape[0]):
            queries[at] = made[:, at * LANES : (at + 1) * LANES]
        flags_q[...] = query_flags(target_lengths, place * local, local)
        for step in range(4):
            flags_k[step * local : (step + 1) * local] = key_flags(
                source_lengths, (place ^ step) * local, local
            )

    both = jnp.concatenate(
        [pair_weight[:, pair_columns(0, pair)], pair_weight[:, pair_columns(width, pair)]], axis=1
    )
    for step, rows in enumerate((rows_0, rows_1, rows_2, rows_3)):
        start = step * local
        made = dot(rows[...], both).astype(LOW)
        key, value = made[:, :LANES], made[:, LANES:]
        key_ref[start : start + local] = key
        value_ref[start : start + local] = value
        widen_pair(key, value, flags_k[start : start + local], key_aug, value_aug, start)
    query = queries[pair].astype(FULL)
    mixed, kept = attend_pair(query * score_scale, flags_q[...], key_aug, value_aug, segments)
    mix_ref[...] = mixed
    query_ref[0] = kept[0]
    query_ref[1] = kept[1]


gelu_factor = 0.7978845608028654
gelu_cubic = 0.044715


def gelu_and_slope(hidden):
    square = hidden * hidden
    bend = jnp.tanh(gelu_factor * (hidden + gelu_cubic * (square * hidden)))
    half = 0.5 * (1.0 + bend)
    slope = half + (0.5 * hidden) * (1.0 - bend * bend) * (
        gelu_factor * (1.0 + (3.0 * gelu_cubic) * square)
    )
    return hidden * half, slope


def middle_kernel(info, mix, first_unit, norms, out_grad, *refs):
    quarters = refs[:8]
    (
        output_ref,
        second_grad_ref,
        mix_grad_ref,
        norm_sums_ref,
        kept,
        sent,
        out_weight,
        expand,
        contract,
        active,
        slope,
        wide_grad,
        tall_grad,
        out_weight_grad,
    ) = refs[8:]
    home = info[0]
    width = mix.shape[1]
    chunks = active.shape[0]
    span = expand.shape[1] // chunks
    fill_weight(out_weight, quarters, home, (0, 1))
    fill_weight(expand, quarters, home, (width, 1))
    fill_weight(contract, quarters, home, (width + expand.shape[1], contract.shape[0] // 512))
    first_norm = first_unit[...] * norms[0:1] + norms[3:4]
    second_unit, second_scale = normalise(first_norm + dot(mix[...], out_weight[...]))
    second_norm = second_unit * norms[1:2] + norms[4:5]
    second_low = second_norm.astype(LOW)

    def forward(at, total):
        start = pl.multiple_of(at * span, span)
        hidden = dot(second_low, expand[:, pl.ds(start, span)])
        made, bent = gelu_and_slope(hidden)
        made = made.astype(LOW)
        active[at] = made
        slope[at] = bent
        return total + dot(made, contract[pl.ds(start, span)])

    mixed = lax.fori_loop(0, chunks, forward, second_norm)
    third_unit, third_scale = normalise(mixed)
    output_ref[...] = third_unit * norms[2:3] + norms[5:6]
    third_grad, gain_three, bias_three = norm_backward(
        out_grad[...], third_unit, third_scale, norms[2:3]
    )
    ffn_grad = third_grad.astype(LOW)
    second_turned = second_low.T

    def backward(at, total):
        start = pl.multiple_of(at * span, span)
        part = contract[pl.ds(start, span)]
        hidden_grad = (dot(ffn_grad, part, BY_LANES) * slope[at]).astype(LOW)
        tall_grad[pl.ds(start, span)] = dot(active[at].T, ffn_grad).astype(LOW)
        wide_grad[:, pl.ds(start, span)] = dot(second_turned, hidden_grad).astype(LOW)
        return total + dot(hidden_grad, expand[:, pl.ds(start, span)], BY_LANES)

    second_cotangent = lax.fori_loop(0, chunks, backward, third_grad)
    second_grad, gain_two, bias_two = norm_backward(
        second_cotangent, second_unit, second_scale, norms[1:2]
    )
    second_grad_ref[...] = second_grad
    cross_out_low = second_grad.astype(LOW)
    mix_grad_ref[...] = dot(cross_out_low, out_weight[...], BY_LANES).astype(LOW)
    out_weight_grad[...] = dot(mix[...].T, cross_out_low).astype(LOW)
    norm_sums_ref[...] = jnp.zeros(norm_sums_ref.shape, FULL)
    norm_sums_ref[1:2] = gain_two
    norm_sums_ref[2:3] = gain_three
    norm_sums_ref[4:5] = bias_two
    norm_sums_ref[5:6] = bias_three
    pack_grad(out_weight_grad, kept, sent, home, (0, 1))
    pack_grad(wide_grad, kept, sent, home, (width, 1))
    pack_grad(tall_grad, kept, sent, home, (width + expand.shape[1], tall_grad.shape[0] // 512))


def attend_back_pair(queries, key, value, flags, mix, grad, segments, key_aug, value_aug, made):
    rows = grad.shape[0]
    keys = key.shape[0]
    lane = lane_numbers((rows, LANES))
    widen_pair(key, value, flags, key_aug, value_aug, 0)
    grad = grad.astype(FULL)
    product = grad * mix.astype(FULL)
    grads = []
    totals = []
    for head in range(2):
        mine = (lane < HEAD_DIM) if head == 0 else (lane >= HEAD_DIM)
        slot = segments + (HEAD_DIM if head == 0 else 0)
        inner = jnp.sum(jnp.where(mine, product, 0.0), axis=1, keepdims=True)
        grads.append(with_parts(jnp.where(mine, grad, 0.0), -inner, lane, slot).astype(LOW))
        totals.append(jnp.zeros((HEAD_DIM, rows), FULL))
    turned = key.T
    lane = lane_numbers((KEY_STEP, LANES))
    for start in range(0, keys, KEY_STEP):
        span = slice(start, start + KEY_STEP)
        key_parts = []
        value_parts = []
        for head in range(2):
            probs = jnp.exp(dot(key_aug[head, span], queries[head], BY_LANES))
            shifted = dot(value_aug[head, span], grads[head], BY_LANES)
            score_grad = (probs * shifted).astype(LOW)
            value_parts.append(dot(probs.astype(LOW), grads[head]))
            key_parts.append(dot(score_grad, queries[head]))
            part = turned[head * HEAD_DIM : (head + 1) * HEAD_DIM, span]
            totals[head] = totals[head] + dot(part, score_grad)
        made[span, :LANES] = jnp.where(lane < HEAD_DIM, key_parts[0], key_parts[1]).astype(LOW)
        made[span, LANES:] = jnp.where(lane < HEAD_DIM, value_parts[0], value_parts[1]).astype(LOW)
    return (jnp.concatenate(totals, axis=0).T * score_scale).astype(LOW)


def cross_backward_kernel(
    info, source_lengths, queries, key, value, mix, grad, rows_0, rows_1, rows_2, rows_3, *refs
):
    quarters = refs[:8]
    (
        query_grad_ref,
        weight_grad_ref,
        own_ref,
        parts_ref,
        weight,
        flags_k,
        key_aug,
        value_aug,
        made,
    ) = refs[8:]
    pair = pl.program_id(0)
    home, place = info[0], info[1]
    local, width = rows_0.shape
    pairs = made.shape[0]
    segments = source_lengths.shape[1] + 1

    @pl.when(pair == 0)
    def _():
        fill_weight(weight, quarters, home, (2 * width, 1))
        for step in range(4):
            flags_k[step * local : (step + 1) * local] = key_flags(
                source_lengths, (place ^ step) * local, local
            )

    query_grad_ref[...] = attend_back_pair(
        queries, key[...], value[...], flags_k[...], mix[...], grad[...], segments, key_aug, value_aug, made.at[pair]
    )

    @pl.when(pair == pairs - 1)
    def _():
        finish_rows(made, weight, 0, (rows_0, rows_1, rows_2, rows_3), own_ref, parts_ref, weight_grad_ref, 0)


def finish_rows(made, weight, first, row_refs, own_ref, parts_ref, weight_grad_ref, grad_first):
    local, width = row_refs[0].shape
    pairs = made.shape[0]
    turned = [rows[...].T for rows in row_refs]
    for step in range(4):
        total = None
        for pair in range(pairs):
            at = first + pair * LANES
            columns = jnp.concatenate(
                [weight[:, at : at + LANES], weight[:, width + at : width + at + LANES]], axis=1
            )
            term = dot(made[pair, step * local : (step + 1) * local], columns, BY_LANES)
            total = term if total is None else total + term
        if step == 0:
            own_ref[...] = total
        else:
            parts_ref[step - 1] = total.astype(LOW)
    for pair in range(pairs):
        total = None
        for step in range(4):
            term = dot(turned[step], made[pair, step * local : (step + 1) * local])
            total = term if total is None else total + term
        at = grad_first + pair * LANES
        weight_grad_ref[:, at : at + LANES] = total[:, :LANES].astype(LOW)
        weight_grad_ref[:, width + at : width + at + LANES] = total[:, LANES:].astype(LOW)


def between_kernel(
    info, query_grad, second_grad, first_unit, first_scale, norms, norm_sums, self_mix, pair_grad, *refs
):
    quarters = refs[:8]
    (
        first_grad_ref,
        mix_grad_ref,
        kept,
        sent,
        out_weight,
        query_weight,
        out_grad,
        query_weight_grad,
        norm_grad,
        norm_rows,
    ) = refs[8:]
    home = info[0]
    width = self_mix.shape[1]
    fill_weight(out_weight, quarters, home, (0, 1))
    fill_weight(query_weight, quarters, home, (width, 1))
    unit = first_unit[...]
    first_low = (unit * norms[0:1] + norms[3:4]).astype(LOW)
    low_grad = query_grad[...]
    query_weight_grad[...] = dot(first_low.T, low_grad).astype(LOW)
    cotangent = second_grad[...] + dot(low_grad, query_weight[...], BY_LANES)
    first_grad, gain_one, bias_one = norm_backward(
        cotangent, unit, first_scale[:, 0:1], norms[0:1]
    )
    first_grad_ref[...] = first_grad
    self_out_low = first_grad.astype(LOW)
    out_grad[...] = dot(self_mix[...].T, self_out_low).astype(LOW)
    mix_grad_ref[...] = dot(self_out_low, out_weight[...], BY_LANES).astype(LOW)
    norm_rows[...] = jnp.zeros(norm_rows.shape, FULL)
    norm_rows[0:8] = norm_sums[...]
    norm_rows[0:1] = gain_one
    norm_rows[3:4] = bias_one
    norm_grad[...] = norm_rows[...].T.astype(LOW)
    pack_grad(out_grad, kept, sent, home, (0, 1))
    pack_grad(query_weight_grad, kept, sent, home, (width, 1))
    pack_grad(pair_grad, kept, sent, home, (2 * width, 1))
    pack_grad(norm_grad, kept, sent, home, (4 * width, 1))


def self_backward_kernel(
    info, lengths, queries, key, value, mix, grad, first_grad, rows_0, rows_1, rows_2, rows_3, *refs
):
    quarters = refs[:8]
    (
        own_ref,
        parts_ref,
        kept,
        sent,
        weight,
        flags_k,
        key_aug,
        value_aug,
        made,
        query_grads,
        weight_grad,
    ) = refs[8:]
    pair = pl.program_id(0)
    home, place = info[0], info[1]
    local, width = rows_0.shape
    pairs = made.shape[0]
    segments = lengths.shape[1] + 1

    @pl.when(pair == 0)
    def _():
        fill_weight(weight, quarters, home, (0, 1))
        for step in range(4):
            flags_k[step * local : (step + 1) * local] = key_flags(
                lengths, (place ^ step) * local, local
            )

    query_grads[pair] = attend_back_pair(
        queries, key[...], value[...], flags_k[...], mix[...], grad[...], segments, key_aug, value_aug, made.at[pair]
    )

    @pl.when(pair == pairs - 1)
    def _():
        finish_rows(
            made, weight, width, (rows_0, rows_1, rows_2, rows_3), own_ref, parts_ref, weight_grad, width
        )
        low_grad = jnp.concatenate([query_grads[at] for at in range(pairs)], axis=1)
        weight_grad[:, 0:width] = dot(rows_0[...].T, low_grad).astype(LOW)
        own_ref[...] += first_grad[...] + dot(low_grad, weight[:, 0:width], BY_LANES)
        pack_grad(weight_grad, kept, sent, home, (0, 1))


def whole(shape):
    return pl.BlockSpec(shape, lambda *at: (0,) * len(shape))


def call(kernel, inputs, specs, outputs, out_specs, scratch, grid=(), flops=0):
    moved = sum(a.size * a.dtype.itemsize for a in inputs) + sum(
        a.size * a.dtype.itemsize for a in outputs
    )
    return pl.pallas_call(
        kernel,
        out_shape=outputs,
        grid=grid,
        in_specs=specs,
        out_specs=out_specs,
        scratch_shapes=scratch,
        compiler_params=pltpu.CompilerParams(vmem_limit_bytes=VMEM_BYTES),
        cost_estimate=pl.CostEstimate(flops=flops, bytes_accessed=moved, transcendentals=0),
    )(*inputs)


SCALARS = pl.BlockSpec(memory_space=pltpu.SMEM)


def shaped(shape, kind):
    return jax.ShapeDtypeStruct(shape, kind)


def per_device(
    target_states,
    memory,
    target_lengths,
    source_lengths,
    self_project,
    self_output,
    cross_project,
    memory_project,
    cross_output,
    expand_weight,
    contract_weight,
    norm_gain,
    norm_bias,
    out_grad,
):
    _, local, width = target_states.shape
    states = target_states[0]
    own_memory = memory[0]
    rows = self_project.shape[0]
    ff = expand_weight.shape[1]
    keys = local * 4
    pairs = width // LANES
    scores = 2 * local * keys * width * 4
    info = jnp.stack([home_number(), lax.axis_index("narrow")]).astype(jnp.int32)

    norm_shard = jnp.concatenate([norm_gain, norm_bias], axis=0).T
    norm_shard = jnp.pad(norm_shard, ((0, 0), (0, LANES - norm_shard.shape[1])))
    batch_1 = self_project
    batch_2 = jnp.concatenate([self_output, cross_project, memory_project, norm_shard], axis=1)
    batch_3 = jnp.concatenate(
        [cross_output, expand_weight, fold_rows(contract_weight, rows)], axis=1
    )
    far_1 = gather_far(batch_1)
    states_x = exchange(states, 2)
    states_c = exchange(states, 1)
    far_2 = gather_far(batch_2)
    plane_1 = gather_plane(far_1)
    far_3 = gather_far(batch_3)
    states_xc = exchange(states_x, 1)
    weights_1 = gather_core(plane_1)
    row_states = [states, states_c, states_x, states_xc]

    plane_2 = gather_plane(far_2)
    memory_x = exchange(own_memory, 2)
    memory_c = exchange(own_memory, 1)

    row_spec = whole((local, width))
    pair_rows = pl.BlockSpec((local, LANES), lambda pair: (0, pair))
    pair_keys = pl.BlockSpec((keys, LANES), lambda pair: (0, pair))
    pair_heads = pl.BlockSpec((2, local, LANES), lambda pair: (pair, 0, 0))
    quarter_specs_1 = [whole(q.shape) for q in weights_1]
    attend_scratch = [
        pltpu.VMEM((local, LANES), FULL),
        pltpu.VMEM((keys, LANES), LOW),
        pltpu.VMEM((2, keys, LANES), LOW),
        pltpu.VMEM((2, keys, LANES), LOW),
    ]
    self_mix, self_queries, self_key, self_value = call(
        self_forward_kernel,
        [info, target_lengths, *row_states, *weights_1],
        [SCALARS, SCALARS] + [row_spec] * 4 + quarter_specs_1,
        [
            shaped((local, width), LOW),
            shaped((2 * pairs, local, LANES), LOW),
            shaped((keys, width), LOW),
            shaped((keys, width), LOW),
        ],
        [pair_rows, pair_heads, pair_keys, pair_keys],
        [pltpu.VMEM((width, 3 * width), LOW)] + attend_scratch,
        grid=(pairs,),
        flops=scores * 3,
    )

    memory_xc = exchange(memory_x, 1)
    weights_2 = gather_core(plane_2)
    row_memory = [own_memory, memory_c, memory_x, memory_xc]
    plane_3 = gather_plane(far_3)
    quarter_specs_2 = [whole(q.shape) for q in weights_2]
    cross_mix, cross_queries, cross_key, cross_value, first_unit, first_scale, norms = call(
        cross_forward_kernel,
        [info, target_lengths, source_lengths, self_mix, states, *row_memory, *weights_2],
        [SCALARS] * 3 + [row_spec] * 6 + quarter_specs_2,
        [
            shaped((local, width), LOW),
            shaped((2 * pairs, local, LANES), LOW),
            shaped((keys, width), LOW),
            shaped((keys, width), LOW),
            shaped((local, width), FULL),
            shaped((local, LANES), FULL),
            shaped((8, width), FULL),
        ],
        [
            pair_rows,
            pair_heads,
            pair_keys,
            pair_keys,
            row_spec,
            whole((local, LANES)),
            whole((8, width)),
        ],
        [
            pltpu.VMEM((width, width), LOW),
            pltpu.VMEM((width, width), LOW),
            pltpu.VMEM((width, 2 * width), LOW),
            pltpu.VMEM((width, LANES), LOW),
            pltpu.VMEM((pairs, local, LANES), LOW),
        ]
        + attend_scratch,
        grid=(pairs,),
        flops=scores * 3,
    )

    weights_3 = gather_core(plane_3, ff // width)
    quarter_specs_3 = [whole(q.shape) for q in weights_3]
    columns_3 = width + 2 * ff
    chunk_count = ff // 512
    packed_3 = (4, 4, TILE_ROWS, columns_3)
    output, second_grad, cross_mix_grad, norm_sums, kept_3, sent_3 = call(
        middle_kernel,
        [info, cross_mix, first_unit, norms, out_grad[0], *weights_3],
        [SCALARS, row_spec, row_spec, whole((8, width)), row_spec] + quarter_specs_3,
        [
            shaped((local, width), FULL),
            shaped((local, width), FULL),
            shaped((local, width), LOW),
            shaped((8, width), FULL),
            shaped(packed_3, LOW),
            shaped(packed_3, LOW),
        ],
        [
            row_spec,
            row_spec,
            row_spec,
            whole((8, width)),
            whole(packed_3),
            whole(packed_3),
        ],
        [
            pltpu.VMEM((width, width), LOW),
            pltpu.VMEM((width, ff), LOW),
            pltpu.VMEM((ff, width), LOW),
            pltpu.VMEM((chunk_count, local, 512), LOW),
            pltpu.VMEM((chunk_count, local, 512), FULL),
            pltpu.VMEM((width, ff), LOW),
            pltpu.VMEM((ff, width), LOW),
            pltpu.VMEM((width, width), LOW),
        ],
        flops=2 * local * width * ff * 6,
    )
    core_3 = reduce_core(kept_3, sent_3)

    back_scratch = [
        pltpu.VMEM((keys, LANES), LOW),
        pltpu.VMEM((2, keys, LANES), LOW),
        pltpu.VMEM((2, keys, LANES), LOW),
        pltpu.VMEM((pairs, keys, 2 * LANES), LOW),
    ]
    parts_shape = (3, local, width)
    cross_query_grad, pair_weight_grad, memory_own, memory_parts = call(
        cross_backward_kernel,
        [
            info,
            source_lengths,
            cross_queries,
            cross_key,
            cross_value,
            cross_mix,
            cross_mix_grad,
            *row_memory,
            *weights_2,
        ],
        [SCALARS] * 2
        + [pair_heads, pair_keys, pair_keys, pair_rows, pair_rows]
        + [row_spec] * 4
        + quarter_specs_2,
        [
            shaped((local, width), LOW),
            shaped((width, 2 * width), LOW),
            shaped((local, width), FULL),
            shaped(parts_shape, LOW),
        ],
        [pair_rows, whole((width, 2 * width)), row_spec, whole(parts_shape)],
        [pltpu.VMEM((width, 2 * width), LOW)] + back_scratch,
        grid=(pairs,),
        flops=scores * 5,
    )
    plane_sum_3 = reduce_plane(core_3)
    memory_grad = reduce_row(memory_own, memory_parts)

    packed_2 = (4, 4, TILE_ROWS, 4 * width + LANES)
    first_grad, self_mix_grad, kept_2, sent_2 = call(
        between_kernel,
        [
            info,
            cross_query_grad,
            second_grad,
            first_unit,
            first_scale,
            norms,
            norm_sums,
            self_mix,
            pair_weight_grad,
            *weights_2,
        ],
        [SCALARS, row_spec, row_spec, row_spec, whole((local, LANES))]
        + [whole((8, width))] * 2
        + [row_spec, whole((width, 2 * width))]
        + quarter_specs_2,
        [
            shaped((local, width), FULL),
            shaped((local, width), LOW),
            shaped(packed_2, LOW),
            shaped(packed_2, LOW),
        ],
        [row_spec, row_spec, whole(packed_2), whole(packed_2)],
        [
            pltpu.VMEM((width, width), LOW),
            pltpu.VMEM((width, width), LOW),
            pltpu.VMEM((width, width), LOW),
            pltpu.VMEM((width, width), LOW),
            pltpu.VMEM((width, LANES), LOW),
            pltpu.VMEM((LANES, width), FULL),
        ],
        flops=2 * local * width * width * 4,
    )
    core_2 = reduce_core(kept_2, sent_2)

    packed_1 = (4, 4, TILE_ROWS, 3 * width)
    states_own, states_parts, kept_1, sent_1 = call(
        self_backward_kernel,
        [
            info,
            target_lengths,
            self_queries,
            self_key,
            self_value,
            self_mix,
            self_mix_grad,
            first_grad,
            *row_states,
            *weights_1,
        ],
        [SCALARS] * 2
        + [pair_heads, pair_keys, pair_keys, pair_rows, pair_rows]
        + [row_spec] * 5
        + quarter_specs_1,
        [
            shaped((local, width), FULL),
            shaped(parts_shape, LOW),
            shaped(packed_1, LOW),
            shaped(packed_1, LOW),
        ],
        [row_spec, whole(parts_shape), whole(packed_1), whole(packed_1)],
        [pltpu.VMEM((width, 3 * width), LOW)]
        + back_scratch
        + [pltpu.VMEM((pairs, local, LANES), LOW), pltpu.VMEM((width, 3 * width), LOW)],
        grid=(pairs,),
        flops=scores * 5,
    )
    core_1 = reduce_core(kept_1, sent_1)
    plane_sum_1 = reduce_plane(core_1)
    plane_sum_2 = reduce_plane(core_2)
    states_grad = reduce_row(states_own, states_parts)
    grad_3 = reduce_far(plane_sum_3, ff // width)
    grad_2 = reduce_far(plane_sum_2)
    grad_1 = reduce_far(plane_sum_1)
    count = norm_gain.shape[0]
    norm_grads = grad_2[:, 4 * width :].T
    return (
        output[None],
        states_grad[None],
        memory_grad[None],
        grad_1,
        grad_2[:, :width],
        grad_2[:, width : 2 * width],
        grad_2[:, 2 * width : 4 * width],
        grad_3[:, :width],
        grad_3[:, width : width + ff],
        unfold_rows(grad_3[:, width + ff :], width),
        norm_grads[:count],
        norm_grads[count : 2 * count],
    )


def reduce_row(own, parts):
    from_core = exchange(parts[0], 1)
    from_far = exchange(parts[2], 1)
    other = (parts[1].astype(FULL) + from_far.astype(FULL)).astype(LOW)
    return own + from_core.astype(FULL) + exchange(other, 2).astype(FULL)


def solution(mesh):
    in_specs = (
        P("wide", "narrow", None),
        P("wide", "narrow", None),
        P("wide", None),
        P("wide", None),
        P(("wide", "narrow"), None),
        P(("wide", "narrow"), None),
        P(("wide", "narrow"), None),
        P(("wide", "narrow"), None),
        P(("wide", "narrow"), None),
        P(("wide", "narrow"), None),
        P(("wide", "narrow"), None),
        P(None, ("wide", "narrow")),
        P(None, ("wide", "narrow")),
        P("wide", "narrow", None),
    )
    out_specs = (
        P("wide", "narrow", None),
        P("wide", "narrow", None),
        P("wide", "narrow", None),
        P(("wide", "narrow"), None),
        P(("wide", "narrow"), None),
        P(("wide", "narrow"), None),
        P(("wide", "narrow"), None),
        P(("wide", "narrow"), None),
        P(("wide", "narrow"), None),
        P(("wide", "narrow"), None),
        P(None, ("wide", "narrow")),
        P(None, ("wide", "narrow")),
    )
    return jax.shard_map(
        per_device, mesh=mesh, in_specs=in_specs, out_specs=out_specs, check_vma=False
    )
```

time: 1930 us -> 337 us (0.17)
  waiting for transfers between devices: 1290 us -> 107 us
  matrix products: 307 us -> 0 us
  blocking collectives: 200 us -> 0 us
  Pallas kernels: 0 us -> 139 us
  starting transfers between devices: 0.94 us -> 57.6 us
  local copies, waits for them, and re-layouts: 71 us -> 15.8 us
  other arithmetic: 34.7 us -> 11.6 us
    reduce_scatter x7 -> x0, waiting for transfers between devices: 683 us -> none  [the longest x1 140 us: settle_grads(): lax.psum_scatter(contract_grad, ('wide', 'narrow'), scatter_dimension=0,...]
    unnamed x21 -> x0, waiting for transfers between devices: 499 us -> none
    dot_general x134 -> x0, matrix products: 307 us -> none  [the longest x32 73.2 us: one_head(): jnp.einsum('rqd,rkd->rqk', query_head, key_head, preferred_element_type=j...]
    all_gather x5 -> x0, blocking collectives: 200 us -> none  [the longest x1 42.7 us: fetch_weights(): lax.all_gather(cross_output, ('wide', 'narrow'), axis=0, tiled=True)]
    pallas_call x0 -> x6, Pallas kernels: none -> 139 us  [call(): pl.pallas_call(kernel, out_shape=outputs, grid=grid, in_specs=specs, out_...]
    all_gather x6 -> x0, waiting for transfers between devices: 112 us -> none  [the longest x1 58.5 us: fetch_weights(): lax.all_gather(memory_project, ('wide', 'narrow'), axis=0, tiled=True)]
    ppermute x0 -> x63, waiting for transfers between devices: none -> 107 us  [exchange(): return lax.ppermute(block, AXES, pairs)]
    ppermute x0 -> x63, starting transfers between devices: none -> 57.6 us  [exchange(): return lax.ppermute(block, AXES, pairs)]
  transfers between devices with their start and end apart: 17 -> 63, of which waited for: 12 -> 23; matrix products, arithmetic and copies ran while one was open for 15% -> 6% of each run, Pallas kernels for 0% -> 14%
where the time goes in v2:
time: 337 us; the launch traced here: 333 us
  Pallas kernels  139 us (41%)
  waiting for transfers between devices  107 us (32%)
  starting transfers between devices  57.6 us (17%)
  local copies, waits for them, and re-layouts  15.8 us (5%)
  other arithmetic  11.6 us (3%)
    pallas_call x6, Pallas kernels, call(): pl.pallas_call(kernel, out_shape=outputs, grid=grid, in_specs=specs, out_...  139 us
    ppermute x63, waiting for transfers between devices, exchange(): return lax.ppermute(block, AXES, pairs)  107 us
    ppermute x63, starting transfers between devices, exchange(): return lax.ppermute(block, AXES, pairs)  57.6 us
    unnamed x69, local copies, waits for them, and re-layouts  9.14 us
  transfers between devices with their start and end apart: 63, of which 23 were waited for; matrix products, arithmetic and copies ran while one was open for 6% of the time, Pallas kernels for 14%

profile of v2, /device:TPU:0, one launch (start us, length us, event | category | flops | bytes accessed | tf_op | source)
XLA Modules:
  0.0 333.0 jit_solution(6660663945132637310)
XLA Ops:
  0.7 3.1 collective-permute-start.3
  3.7 2.5 collective-permute-start.5
  8.7 1.8 collective-permute-start.16
  10.5 2.5 collective-permute-start.18
  14.5 0.8 constant_dynamic-update-slice_fusion
  18.2 2.1 collective-permute-start.28
  20.4 1.2 collective-permute-start.27
  21.7 1.1 collective-permute-start.26
  22.8 5.5 %collective-permute-done.4 = bf16[16,1536]{1,0:T(8,128)(2,1)S(1)} collective-permute-done((bf16[16,1536]{1,0:T(8,128)(2,1)}, bf16[16,1536]{1,0:T(8,128)(2,1)S(1)}, u32[]{:S(2)}, u32[]{:S(2)}) %collective-permute-start.4) | collective-permute-done | bytes 49184 | tf_op jit(solution)/shard_map/ppermute | solution.py:34
  29.2 2.5 collective-permute-start.8
  31.7 2.8 collective-permute-done.27
  34.6 1.5 collective-permute-start.7
  36.1 1.5 collective-permute-start.6
  38.1 3.6 %collective-permute-done.7.refs_2_ = bf16[4,16,1536]{2,1,0:T(8,128)(2,1)} collective-permute-done((bf16[4,16,1536]{2,1,0:T(8,128)(2,1)S(1)}, bf16[4,16,1536]{2,1,0:T(8,128)(2,1)}, u32[]{:S(2)}, u32[]{:S(2)}) %collective-permute-start.7) | collective-permute-done | bytes 196640 | tf_op jit(solution)/shard_map/ppermute | solution.py:34
  41.8 2.4 collective-permute-start.21
  44.7 1.3 collective-permute-start.19
  46.0 15.0 %collective-permute-done.21.refs_3_ = bf16[4,16,2176]{2,1,0:T(8,128)(2,1)S(1)} collective-permute-done((bf16[4,16,2176]{2,1,0:T(8,128)(2,1)S(1)}, bf16[4,16,2176]{2,1,0:T(8,128)(2,1)S(1)}, u32[]{:S(2)}, u32[]{:S(2)}) %collective-permute-start.21) | collective-permute-done | bytes 278560 | tf_op jit(solution)/shard_map/ppermute | solution.py:34
  61.6 3.4 %collective-permute-done.19.refs_1_ = bf16[4,16,2176]{2,1,0:T(8,128)(2,1)S(1)} collective-permute-done((bf16[4,16,2176]{2,1,0:T(8,128)(2,1)S(1)}, bf16[4,16,2176]{2,1,0:T(8,128)(2,1)S(1)}, u32[]{:S(2)}, u32[]{:S(2)}) %collective-permute-start.19) | collective-permute-done | bytes 278560 | tf_op jit(solution)/shard_map/ppermute | solution.py:34
  65.6 1.5 collective-permute-start.14
  68.2 11.8 %collective-permute-done.14.rows_2 = bf16[512,512]{1,0:T(8,128)(2,1)} collective-permute-done((bf16[512,512]{1,0:T(8,128)(2,1)S(1)}, bf16[512,512]{1,0:T(8,128)(2,1)}, u32[]{:S(2)}, u32[]{:S(2)}) %collective-permute-start.14) | collective-permute-done | bytes 524320 | tf_op jit(solution)/shard_map/ppermute | solution.py:34
  80.0 1.4 collective-permute-start.31
  81.4 1.5 collective-permute-start.30
  84.9 23.1 %shard_map.229 = (bf16[512,512]{1,0:T(8,128)(2,1)}, bf16[8,512,128]{2,1,0:T(8,128)(2,1)}, bf16[2048,512]{1,0:T(8,128)(2,1)}, bf16[2048,512]{1,0:T(8,128)(2,1)}) custom-call(s32[2]{0:T(128)} %pad_add_fusion.info, s32[1,16]{1,0:T(1,128)} %lengths.3, bf16[512,512]{1,0:T(8,128)(2,1)} %bitcast.125, bf16[512,512]{1,0:T(8,128)(2,1)} %collective-permute-done.rows_1, ...), custom_call_target="tpu_custom_call" | custom-call | flops 12884901888 | bytes 9437256 | tf_op jit(solution)/shard_map/pallas_call | solution.py:663
  109.2 24.6 %shard_map.230 = (bf16[512,512]{1,0:T(8,128)(2,1)}, bf16[8,512,128]{2,1,0:T(8,128)(2,1)}, bf16[2048,512]{1,0:T(8,128)(2,1)}, bf16[2048,512]{1,0:T(8,128)(2,1)}, ...) custom-call(s32[2]{0:T(128)} %pad_add_fusion.info, s32[1,16]{1,0:T(1,128)} %lengths.3, ...), custom_call_target="tpu_custom_call" | custom-call | flops 12884901888 | bytes 12468360 | tf_op jit(solution)/shard_map/pallas_call | solution.py:663
  135.3 19.2 %shard_map.231 = (f32[512,512]{1,0:T(8,128)}, f32[512,512]{1,0:T(8,128)}, bf16[512,512]{1,0:T(8,128)(2,1)}, f32[8,512]{1,0:T(8,128)}, bf16[4,4,16,4608]{3,2,1,0:...) custom-call(s32[2]{0:T(128)} %pad_add_fusion.info, bf16[512,512]{1,0:T(8,128)(2,1)} %get-tuple-element.42.mix, ...), custom_call_target="tpu_custom_call" | custom-call | flops 6442450944 | bytes 14712840 | tf_op jit(solution)/shard_map/pallas_call | solution.py:663
  154.5 32.4 %shard_map.232 = (bf16[512,512]{1,0:T(8,128)(2,1)}, bf16[512,1024]{1,0:T(8,128)(2,1)}, f32[512,512]{1,0:T(8,128)}, bf16[3,512,512]{2,1,0:T(8,128)(2,1)}) custom-call(s32[2]{0:T(128)} %pad_add_fusion.info, s32[1,16]{1,0:T(1,128)} %source_lengths.3, bf16[8,512,128]{2,1,0:T(8,128)(2,1)} %get-tuple-element.49.queries, bf16[2048,512]{1,0:T(8,128)(2,1)} %get-tuple-element.50.key, ...), custom_call_target="tpu_custom_call" | custom-call | flops 21474836480 | bytes 14811208 | tf_op jit(solution)/shard_map/pallas_call | solution.py:663
  186.9 6.3 %shard_map.233 = (f32[512,512]{1,0:T(8,128)}, bf16[512,512]{1,0:T(8,128)(2,1)}, bf16[4,4,16,2176]{3,2,1,0:T(8,128)(2,1)}, bf16[4,4,16,2176]{3,2,1,0:T(8,128)(2,1)}) custom-call(s32[2]{0:T(128)} %pad_add_fusion.info, bf16[512,512]{1,0:T(8,128)(2,1)} %get-tuple-element.53.query_grad, f32[512,512]{1,0:T(8,128)} %get-tuple-element.54.second_grad, ...), custom_call_target="tpu_custom_call" | custom-call | flops 1073741824 | bytes 10518536 | tf_op jit(solution)/shard_map/pallas_call | solution.py:663
  193.3 33.7 %shard_map.234 = (f32[512,512]{1,0:T(8,128)}, bf16[3,512,512]{2,1,0:T(8,128)(2,1)}, bf16[4,4,16,1536]{3,2,1,0:T(8,128)(2,1)}, bf16[4,4,16,1536]{3,2,1,0:T(8,128)(2,1)}) custom-call(s32[2]{0:T(128)} %pad_add_fusion.info, s32[1,16]{1,0:T(1,128)} %lengths.3, bf16[8,512,128]{2,1,0:T(8,128)(2,1)} %get-tuple-element.46.queries, ...), custom_call_target="tpu_custom_call" | custom-call | flops 21474836480 | bytes 15204424 | tf_op jit(solution)/shard_map/pallas_call | solution.py:663
  227.2 1.3 slice_bitcast_fusion.7
  229.9 1.6 collective-permute-start.43
  232.0 1.5 collective-permute-start.44
  233.5 4.2 %collective-permute-done.43 = bf16[4,16,1536]{2,1,0:T(8,128)(2,1)S(1)} collective-permute-done((bf16[4,16,1536]{2,1,0:T(8,128)(2,1)S(1)}, bf16[4,16,1536]{2,1,0:T(8,128)(2,1)S(1)}, u32[]{:S(2)}, u32[]{:S(2)}) %collective-permute-start.43) | collective-permute-done | bytes 196640 | tf_op jit(solution)/shard_map/ppermute | solution.py:34
  237.7 3.5 %collective-permute-done.45 = bf16[4,16,1536]{2,1,0:T(8,128)(2,1)S(1)} collective-permute-done((bf16[4,16,1536]{2,1,0:T(8,128)(2,1)S(1)}, bf16[4,16,1536]{2,1,0:T(8,128)(2,1)S(1)}, u32[]{:S(2)}, u32[]{:S(2)}) %collective-permute-start.45) | collective-permute-done | bytes 196640 | tf_op jit(solution)/shard_map/ppermute | solution.py:34
  241.2 1.4 collective-permute-done.44
  242.7 1.8 collective-permute-start.46
  244.5 1.2 fusion.4
  245.6 1.2 collective-permute-start.38
  246.9 2.0 collective-permute-start.48
  249.4 3.3 %collective-permute-done.48 = bf16[16,1536]{1,0:T(8,128)(2,1)S(1)} collective-permute-done((bf16[16,1536]{1,0:T(8,128)(2,1)S(1)}, bf16[16,1536]{1,0:T(8,128)(2,1)S(1)}, u32[]{:S(2)}, u32[]{:S(2)}) %collective-permute-start.48) | collective-permute-done | bytes 49184 | tf_op jit(solution)/shard_map/ppermute | solution.py:34
  252.8 1.1 collective-permute-done.47
  255.4 3.7 %collective-permute-done.38 = bf16[512,512]{1,0:T(8,128)(2,1)S(1)} collective-permute-done((bf16[512,512]{1,0:T(8,128)(2,1)S(1)}, bf16[512,512]{1,0:T(8,128)(2,1)S(1)}, u32[]{:S(2)}, u32[]{:S(2)}) %collective-permute-start.38) | collective-permute-done | bytes 524320 | tf_op jit(solution)/shard_map/ppermute | solution.py:34
  259.1 1.2 add_bitcast_fusion.1
  260.9 1.7 collective-permute-start.50
  262.5 1.0 collective-permute-start.52
  263.6 0.8 collective-permute-start.51
  264.4 5.9 %collective-permute-done.41 = bf16[512,512]{1,0:T(8,128)(2,1)S(1)} collective-permute-done((bf16[512,512]{1,0:T(8,128)(2,1)S(1)}, bf16[512,512]{1,0:T(8,128)(2,1)S(1)}, u32[]{:S(2)}, u32[]{:S(2)}) %collective-permute-start.41) | collective-permute-done | bytes 524320 | tf_op jit(solution)/shard_map/ppermute | solution.py:34
  270.3 1.2 add_bitcast_fusion
  271.5 4.7 %collective-permute-done.50 = bf16[4,16,2176]{2,1,0:T(8,128)(2,1)S(1)} collective-permute-done((bf16[4,16,2176]{2,1,0:T(8,128)(2,1)S(1)}, bf16[4,16,2176]{2,1,0:T(8,128)(2,1)S(1)}, u32[]{:S(2)}, u32[]{:S(2)}) %collective-permute-start.50) | collective-permute-done | bytes 278560 | tf_op jit(solution)/shard_map/ppermute | solution.py:34
  276.3 6.0 %collective-permute-done.52 = bf16[4,16,2176]{2,1,0:T(8,128)(2,1)S(1)} collective-permute-done((bf16[4,16,2176]{2,1,0:T(8,128)(2,1)S(1)}, bf16[4,16,2176]{2,1,0:T(8,128)(2,1)S(1)}, u32[]{:S(2)}, u32[]{:S(2)}) %collective-permute-start.52) | collective-permute-done | bytes 278560 | tf_op jit(solution)/shard_map/ppermute | solution.py:34
  282.4 0.9 collective-permute-start.53
  283.3 2.3 collective-permute-start.55
  286.7 1.0 slice_bitcast_fusion.2
  287.7 1.5 collective-permute-start.57
  290.0 1.2 collective-permute-start.58
  291.2 1.0 collective-permute-done.54
  294.3 10.0 %collective-permute-done.57 = bf16[4,16,4608]{2,1,0:T(8,128)(2,1)} collective-permute-done((bf16[4,16,4608]{2,1,0:T(8,128)(2,1)}, bf16[4,16,4608]{2,1,0:T(8,128)(2,1)}, u32[]{:S(2)}, u32[]{:S(2)}) %collective-permute-start.57) | collective-permute-done | bytes 589856 | tf_op jit(solution)/shard_map/ppermute | solution.py:34
  304.3 10.6 %collective-permute-done.59 = bf16[4,16,4608]{2,1,0:T(8,128)(2,1)} collective-permute-done((bf16[4,16,4608]{2,1,0:T(8,128)(2,1)S(1)}, bf16[4,16,4608]{2,1,0:T(8,128)(2,1)}, u32[]{:S(2)}, u32[]{:S(2)}) %collective-permute-start.59) | collective-permute-done | bytes 589856 | tf_op jit(solution)/shard_map/ppermute | solution.py:34
  314.9 1.2 collective-permute-done.58
  316.0 1.7 fusion.2
  317.8 1.3 collective-permute-start.60
  319.1 1.9 collective-permute-start.62
  321.3 1.4 fusion.20
  323.2 2.9 collective-permute-done.62
  326.1 4.6 %collective-permute-done.61 = bf16[16,4608]{1,0:T(8,128)(2,1)S(1)} collective-permute-done((bf16[16,4608]{1,0:T(8,128)(2,1)S(1)}, bf16[16,4608]{1,0:T(8,128)(2,1)S(1)}, u32[]{:S(2)}, u32[]{:S(2)}) %collective-permute-start.61) | collective-permute-done | bytes 147488 | tf_op jit(solution)/shard_map/ppermute | solution.py:34
  (173 shorter events, 27.2 us)
Async XLA Ops:
  0.7 21.0 %collective-permute-start.3 = (bf16[16,1536]{1,0:T(8,128)(2,1)}, bf16[16,1536]{1,0:T(8,128)(2,1)S(1)}, u32[]{:S(2)}, u32[]{:S(2)}) collective-permute-start(bf16[16,1536]{1,0:T(8,128)(2,1)} %param.18), channel_id=1, source_target_pairs={{0,8},{1,9},{2,10},{3,11},{4,12},{5,13},{6,14},{7,15},{8,0},{9,1},... | collective-permute-start | bytes 147464 | tf_op jit(solution)/shard_map/ppermute | solution.py:34
  3.7 19.1 %collective-permute-start.5 = (bf16[16,1536]{1,0:T(8,128)(2,1)}, bf16[16,1536]{1,0:T(8,128)(2,1)S(1)}, u32[]{:S(2)}, u32[]{:S(2)}) collective-permute-start(bf16[16,1536]{1,0:T(8,128)(2,1)} %param.18), channel_id=1, source_target_pairs={{0,24},{1,25},{2,26},{3,27},{4,28},{5,29},{6,30},{7,31},{8,16},{9,... | collective-permute-start | bytes 147464 | tf_op jit(solution)/shard_map/ppermute | solution.py:34
  8.6 9.6 %collective-permute-start.17 = (bf16[16,2176]{1,0:T(8,128)(2,1)S(1)}, bf16[16,2176]{1,0:T(8,128)(2,1)S(1)}, u32[]{:S(2)}, u32[]{:S(2)}) collective-permute-start(bf16[16,2176]{1,0:T(8,128)(2,1)S(1)} %fusion.18), channel_id=1, source_target_pairs={{0,16},{1,17},{2,18},{3,19},{4,20},{5,21},{6,22},{7,23},{8,24},{9,... | collective-permute-start | bytes 208904 | tf_op jit(solution)/shard_map/ppermute | solution.py:34
  8.7 9.5 %collective-permute-start.16 = (bf16[16,2176]{1,0:T(8,128)(2,1)S(1)}, bf16[16,2176]{1,0:T(8,128)(2,1)S(1)}, u32[]{:S(2)}, u32[]{:S(2)}) collective-permute-start(bf16[16,2176]{1,0:T(8,128)(2,1)S(1)} %fusion.18), channel_id=1, source_target_pairs={{0,8},{1,9},{2,10},{3,11},{4,12},{5,13},{6,14},{7,15},{8,0},{9,1},... | collective-permute-start | bytes 208904 | tf_op jit(solution)/shard_map/ppermute | solution.py:34
  10.5 9.8 %collective-permute-start.18 = (bf16[16,2176]{1,0:T(8,128)(2,1)S(1)}, bf16[16,2176]{1,0:T(8,128)(2,1)S(1)}, u32[]{:S(2)}, u32[]{:S(2)}) collective-permute-start(bf16[16,2176]{1,0:T(8,128)(2,1)S(1)} %fusion.18), channel_id=1, source_target_pairs={{0,24},{1,25},{2,26},{3,27},{4,28},{5,29},{6,30},{7,31},{8,16},{9,... | collective-permute-start | bytes 208904 | tf_op jit(solution)/shard_map/ppermute | solution.py:34
  18.2 10.1 %collective-permute-start.4 = (bf16[16,1536]{1,0:T(8,128)(2,1)}, bf16[16,1536]{1,0:T(8,128)(2,1)S(1)}, u32[]{:S(2)}, u32[]{:S(2)}) collective-permute-start(bf16[16,1536]{1,0:T(8,128)(2,1)} %param.18), channel_id=1, source_target_pairs={{0,16},{1,17},{2,18},{3,19},{4,20},{5,21},{6,22},{7,23},{8,24},{9,... | collective-permute-start | bytes 147464 | tf_op jit(solution)/shard_map/ppermute | solution.py:34
  18.2 11.0 %collective-permute-start.28 = (bf16[16,4608]{1,0:T(8,128)(2,1)S(1)}, bf16[16,4608]{1,0:T(8,128)(2,1)S(1)}, u32[]{:S(2)}, u32[]{:S(2)}) collective-permute-start(bf16[16,4608]{1,0:T(8,128)(2,1)S(1)} %slice_dynamic-update-slice_fusion), channel_id=1, source_target_pairs={{0,24},{1,25},{2,26},{3,27},{4,28},{5,29},{6,30},{7,31},{8,16},{9,... | collective-permute-start | bytes 442376 | tf_op jit(solution)/shard_map/ppermute | solution.py:34
  20.4 14.2 %collective-permute-start.27 = (bf16[16,4608]{1,0:T(8,128)(2,1)S(1)}, bf16[16,4608]{1,0:T(8,128)(2,1)S(1)}, u32[]{:S(2)}, u32[]{:S(2)}) collective-permute-start(bf16[16,4608]{1,0:T(8,128)(2,1)S(1)} %slice_dynamic-update-slice_fusion), channel_id=1, source_target_pairs={{0,16},{1,17},{2,18},{3,19},{4,20},{5,21},{6,22},{7,23},{8,24},{9,... | collective-permute-start | bytes 442376 | tf_op jit(solution)/shard_map/ppermute | solution.py:34
  21.6 86.3 %copy-start.3 = (bf16[4,16,2176]{2,1,0:T(8,128)(2,1)}, bf16[4,16,2176]{2,1,0:T(8,128)(2,1)S(1)}, u32[]{:S(2)}) copy-start(bf16[4,16,2176]{2,1,0:T(8,128)(2,1)S(1)} %pad_maximum_fusion.1.refs_0_) | copy-start | bytes 835588
  21.7 14.4 %collective-permute-start.26 = (bf16[16,4608]{1,0:T(8,128)(2,1)S(1)}, bf16[16,4608]{1,0:T(8,128)(2,1)S(1)}, u32[]{:S(2)}, u32[]{:S(2)}) collective-permute-start(bf16[16,4608]{1,0:T(8,128)(2,1)S(1)} %slice_dynamic-update-slice_fusion), channel_id=1, source_target_pairs={{0,8},{1,9},{2,10},{3,11},{4,12},{5,13},{6,14},{7,15},{8,0},{9,1},... | collective-permute-start | bytes 442376 | tf_op jit(solution)/shard_map/ppermute | solution.py:34
  22.8 21.9 %collective-permute-start.22 = (bf16[4,16,2176]{2,1,0:T(8,128)(2,1)S(1)}, bf16[4,16,2176]{2,1,0:T(8,128)(2,1)S(1)}, u32[]{:S(2)}, u32[]{:S(2)}) collective-permute-start(bf16[4,16,2176]{2,1,0:T(8,128)(2,1)S(1)} %pad_maximum_fusion.1.refs_0_), channel_id=1, source_target_pairs={{0,1},{1,0},{2,3},{3,2},{4,5},{5,4},{6,7},{7,6},{8,9},{9,8},{10,11... | collective-permute-start | bytes 835592 | tf_op jit(solution)/shard_map/ppermute | solution.py:34
  29.1 8.4 %collective-permute-start.9 = (bf16[4,16,1536]{2,1,0:T(8,128)(2,1)S(1)}, bf16[4,16,1536]{2,1,0:T(8,128)(2,1)S(1)}, u32[]{:S(2)}, u32[]{:S(2)}) collective-permute-start(bf16[4,16,1536]{2,1,0:T(8,128)(2,1)S(1)} %pad_maximum_fusion.2.refs_0_), channel_id=1, source_target_pairs={{0,1},{1,0},{2,3},{3,2},{4,5},{5,4},{6,7},{7,6},{8,9},{9,8},{10,11... | collective-permute-start | bytes 589832 | tf_op jit(solution)/shard_map/ppermute | solution.py:34
  29.2 8.9 %collective-permute-start.8 = (bf16[4,16,1536]{2,1,0:T(8,128)(2,1)S(1)}, bf16[4,16,1536]{2,1,0:T(8,128)(2,1)}, u32[]{:S(2)}, u32[]{:S(2)}) collective-permute-start(bf16[4,16,1536]{2,1,0:T(8,128)(2,1)S(1)} %pad_maximum_fusion.2.refs_0_), channel_id=1, source_target_pairs={{0,6},{1,7},{2,4},{3,5},{4,2},{5,3},{6,0},{7,1},{8,14},{9,15},{10,... | collective-permute-start | bytes 589832 | tf_op jit(solution)/shard_map/ppermute | solution.py:34
  34.6 7.2 %collective-permute-start.7 = (bf16[4,16,1536]{2,1,0:T(8,128)(2,1)S(1)}, bf16[4,16,1536]{2,1,0:T(8,128)(2,1)}, u32[]{:S(2)}, u32[]{:S(2)}) collective-permute-start(bf16[4,16,1536]{2,1,0:T(8,128)(2,1)S(1)} %pad_maximum_fusion.2.refs_0_), channel_id=1, source_target_pairs={{0,4},{1,5},{2,6},{3,7},{4,0},{5,1},{6,2},{7,3},{8,12},{9,13},{10,... | collective-permute-start | bytes 589832 | tf_op jit(solution)/shard_map/ppermute | solution.py:34
  36.1 8.1 %collective-permute-start.6 = (bf16[4,16,1536]{2,1,0:T(8,128)(2,1)S(1)}, bf16[4,16,1536]{2,1,0:T(8,128)(2,1)}, u32[]{:S(2)}, u32[]{:S(2)}) collective-permute-start(bf16[4,16,1536]{2,1,0:T(8,128)(2,1)S(1)} %pad_maximum_fusion.2.refs_0_), channel_id=1, source_target_pairs={{0,2},{1,3},{2,0},{3,1},{4,6},{5,7},{6,4},{7,5},{8,10},{9,11},{10,... | collective-permute-start | bytes 589832 | tf_op jit(solution)/shard_map/ppermute | solution.py:34
  37.6 30.0 %collective-permute-start.1 = (bf16[512,512]{1,0:T(8,128)(2,1)}, bf16[512,512]{1,0:T(8,128)(2,1)S(1)}, u32[]{:S(2)}, u32[]{:S(2)}) collective-permute-start(bf16[512,512]{1,0:T(8,128)(2,1)} %bitcast.123), channel_id=1, source_target_pairs={{0,2},{1,3},{2,0},{3,1},{4,6},{5,7},{6,4},{7,5},{8,10},{9,11},{10,... | collective-permute-start | bytes 1572872 | tf_op jit(solution)/shard_map/ppermute | solution.py:34
  38.1 29.7 %collective-permute-start = (bf16[512,512]{1,0:T(8,128)(2,1)}, bf16[512,512]{1,0:T(8,128)(2,1)}, u32[]{:S(2)}, u32[]{:S(2)}) collective-permute-start(bf16[512,512]{1,0:T(8,128)(2,1)} %bitcast.124), channel_id=1, source_target_pairs={{0,1},{1,0},{2,3},{3,2},{4,5},{5,4},{6,7},{7,6},{8,9},{9,8},{10,11... | collective-permute-start | bytes 1572872 | tf_op jit(solution)/shard_map/ppermute | solution.py:34
  41.8 19.3 %collective-permute-start.21 = (bf16[4,16,2176]{2,1,0:T(8,128)(2,1)S(1)}, bf16[4,16,2176]{2,1,0:T(8,128)(2,1)S(1)}, u32[]{:S(2)}, u32[]{:S(2)}) collective-permute-start(bf16[4,16,2176]{2,1,0:T(8,128)(2,1)S(1)} %pad_maximum_fusion.1.refs_0_), channel_id=1, source_target_pairs={{0,6},{1,7},{2,4},{3,5},{4,2},{5,3},{6,0},{7,1},{8,14},{9,15},{10,... | collective-permute-start | bytes 835592 | tf_op jit(solution)/shard_map/ppermute | solution.py:34
  44.2 16.9 %collective-permute-start.20 = (bf16[4,16,2176]{2,1,0:T(8,128)(2,1)S(1)}, bf16[4,16,2176]{2,1,0:T(8,128)(2,1)S(1)}, u32[]{:S(2)}, u32[]{:S(2)}) collective-permute-start(bf16[4,16,2176]{2,1,0:T(8,128)(2,1)S(1)} %pad_maximum_fusion.1.refs_0_), channel_id=1, source_target_pairs={{0,4},{1,5},{2,6},{3,7},{4,0},{5,1},{6,2},{7,3},{8,12},{9,13},{10,... | collective-permute-start | bytes 835592 | tf_op jit(solution)/shard_map/ppermute | solution.py:34
  44.7 20.3 %collective-permute-start.19 = (bf16[4,16,2176]{2,1,0:T(8,128)(2,1)S(1)}, bf16[4,16,2176]{2,1,0:T(8,128)(2,1)S(1)}, u32[]{:S(2)}, u32[]{:S(2)}) collective-permute-start(bf16[4,16,2176]{2,1,0:T(8,128)(2,1)S(1)} %pad_maximum_fusion.1.refs_0_), channel_id=1, source_target_pairs={{0,2},{1,3},{2,0},{3,1},{4,6},{5,7},{6,4},{7,5},{8,10},{9,11},{10,... | collective-permute-start | bytes 835592 | tf_op jit(solution)/shard_map/ppermute | solution.py:34
  61.1 4.5 %collective-permute-start.12 = (bf16[4,16,1536]{2,1,0:T(8,128)(2,1)}, bf16[4,16,1536]{2,1,0:T(8,128)(2,1)}, u32[]{:S(2)}, u32[]{:S(2)}) collective-permute-start(bf16[4,16,1536]{2,1,0:T(8,128)(2,1)} %collective-permute-done.8.refs_3_), channel_id=1, source_target_pairs={{0,1},{1,0},{2,3},{3,2},{4,5},{5,4},{6,7},{7,6},{8,9},{9,8},{10,11... | collective-permute-start | bytes 589832 | tf_op jit(solution)/shard_map/ppermute | solution.py:34
  61.1 6.0 %collective-permute-start.11 = (bf16[4,16,1536]{2,1,0:T(8,128)(2,1)}, bf16[4,16,1536]{2,1,0:T(8,128)(2,1)}, u32[]{:S(2)}, u32[]{:S(2)}) collective-permute-start(bf16[4,16,1536]{2,1,0:T(8,128)(2,1)} %collective-permute-done.7.refs_2_), channel_id=1, source_target_pairs={{0,1},{1,0},{2,3},{3,2},{4,5},{5,4},{6,7},{7,6},{8,9},{9,8},{10,11... | collective-permute-start | bytes 589832 | tf_op jit(solution)/shard_map/ppermute | solution.py:34
  65.0 2.3 collective-permute-start.10
  65.6 14.4 %collective-permute-start.14 = (bf16[512,512]{1,0:T(8,128)(2,1)S(1)}, bf16[512,512]{1,0:T(8,128)(2,1)}, u32[]{:S(2)}, u32[]{:S(2)}) collective-permute-start(bf16[512,512]{1,0:T(8,128)(2,1)S(1)} %bitcast.121), channel_id=1, source_target_pairs={{0,2},{1,3},{2,0},{3,1},{4,6},{5,7},{6,4},{7,5},{8,10},{9,11},{10,... | collective-permute-start | bytes 1572872 | tf_op jit(solution)/shard_map/ppermute | solution.py:34
  67.1 14.4 %collective-permute-start.13 = (bf16[512,512]{1,0:T(8,128)(2,1)S(1)}, bf16[512,512]{1,0:T(8,128)(2,1)}, u32[]{:S(2)}, u32[]{:S(2)}) collective-permute-start(bf16[512,512]{1,0:T(8,128)(2,1)S(1)} %bitcast.122), channel_id=1, source_target_pairs={{0,1},{1,0},{2,3},{3,2},{4,5},{5,4},{6,7},{7,6},{8,9},{9,8},{10,11... | collective-permute-start | bytes 1572872 | tf_op jit(solution)/shard_map/ppermute | solution.py:34
  67.3 15.7 %collective-permute-start.25 = (bf16[4,16,2176]{2,1,0:T(8,128)(2,1)S(1)}, bf16[4,16,2176]{2,1,0:T(8,128)(2,1)S(1)}, u32[]{:S(2)}, u32[]{:S(2)}) collective-permute-start(bf16[4,16,2176]{2,1,0:T(8,128)(2,1)S(1)} %collective-permute-done.21.refs_3_), channel_id=1, source_target_pairs={{0,1},{1,0},{2,3},{3,2},{4,5},{5,4},{6,7},{7,6},{8,9},{9,8},{10,11... | collective-permute-start | bytes 835592 | tf_op jit(solution)/shard_map/ppermute | solution.py:34
  67.6 15.9 %collective-permute-start.24 = (bf16[4,16,2176]{2,1,0:T(8,128)(2,1)S(1)}, bf16[4,16,2176]{2,1,0:T(8,128)(2,1)S(1)}, u32[]{:S(2)}, u32[]{:S(2)}) collective-permute-start(bf16[4,16,2176]{2,1,0:T(8,128)(2,1)S(1)} %collective-permute-done.20.refs_2_), channel_id=1, source_target_pairs={{0,1},{1,0},{2,3},{3,2},{4,5},{5,4},{6,7},{7,6},{8,9},{9,8},{10,11... | collective-permute-start | bytes 835592 | tf_op jit(solution)/shard_map/ppermute | solution.py:34
  67.8 15.7 %collective-permute-start.2 = (bf16[512,512]{1,0:T(8,128)(2,1)S(1)}, bf16[512,512]{1,0:T(8,128)(2,1)S(1)}, u32[]{:S(2)}, u32[]{:S(2)}) collective-permute-start(bf16[512,512]{1,0:T(8,128)(2,1)S(1)} %collective-permute-done.1.rows_2), channel_id=1, source_target_pairs={{0,1},{1,0},{2,3},{3,2},{4,5},{5,4},{6,7},{7,6},{8,9},{9,8},{10,11... | collective-permute-start | bytes 1572872 | tf_op jit(solution)/shard_map/ppermute | solution.py:34
  80.0 28.2 %collective-permute-start.31 = (bf16[4,16,4608]{2,1,0:T(8,128)(2,1)S(1)}, bf16[4,16,4608]{2,1,0:T(8,128)(2,1)S(1)}, u32[]{:S(2)}, u32[]{:S(2)}) collective-permute-start(bf16[4,16,4608]{2,1,0:T(8,128)(2,1)S(1)} %pad_maximum_fusion.refs_0_), channel_id=1, source_target_pairs={{0,6},{1,7},{2,4},{3,5},{4,2},{5,3},{6,0},{7,1},{8,14},{9,15},{10,... | collective-permute-start | bytes 1769480 | tf_op jit(solution)/shard_map/ppermute | solution.py:34
  81.4 27.2 %collective-permute-start.30 = (bf16[4,16,4608]{2,1,0:T(8,128)(2,1)S(1)}, bf16[4,16,4608]{2,1,0:T(8,128)(2,1)S(1)}, u32[]{:S(2)}, u32[]{:S(2)}) collective-permute-start(bf16[4,16,4608]{2,1,0:T(8,128)(2,1)S(1)} %pad_maximum_fusion.refs_0_), channel_id=1, source_target_pairs={{0,4},{1,5},{2,6},{3,7},{4,0},{5,1},{6,2},{7,3},{8,12},{9,13},{10,... | collective-permute-start | bytes 1769480 | tf_op jit(solution)/shard_map/ppermute | solution.py:34
  83.0 25.8 %collective-permute-start.29 = (bf16[4,16,4608]{2,1,0:T(8,128)(2,1)S(1)}, bf16[4,16,4608]{2,1,0:T(8,128)(2,1)S(1)}, u32[]{:S(2)}, u32[]{:S(2)}) collective-permute-start(bf16[4,16,4608]{2,1,0:T(8,128)(2,1)S(1)} %pad_maximum_fusion.refs_0_), channel_id=1, source_target_pairs={{0,2},{1,3},{2,0},{3,1},{4,6},{5,7},{6,4},{7,5},{8,10},{9,11},{10,... | collective-permute-start | bytes 1769480 | tf_op jit(solution)/shard_map/ppermute | solution.py:34
  83.5 24.5 %collective-permute-start.23 = (bf16[4,16,2176]{2,1,0:T(8,128)(2,1)S(1)}, bf16[4,16,2176]{2,1,0:T(8,128)(2,1)S(1)}, u32[]{:S(2)}, u32[]{:S(2)}) collective-permute-start(bf16[4,16,2176]{2,1,0:T(8,128)(2,1)S(1)} %collective-permute-done.19.refs_1_), channel_id=1, source_target_pairs={{0,1},{1,0},{2,3},{3,2},{4,5},{5,4},{6,7},{7,6},{8,9},{9,8},{10,11... | collective-permute-start | bytes 835592 | tf_op jit(solution)/shard_map/ppermute | solution.py:34
  84.4 24.8 %collective-permute-start.15 = (bf16[512,512]{1,0:T(8,128)(2,1)}, bf16[512,512]{1,0:T(8,128)(2,1)}, u32[]{:S(2)}, u32[]{:S(2)}) collective-permute-start(bf16[512,512]{1,0:T(8,128)(2,1)} %collective-permute-done.14.rows_2), channel_id=1, source_target_pairs={{0,1},{1,0},{2,3},{3,2},{4,5},{5,4},{6,7},{7,6},{8,9},{9,8},{10,11... | collective-permute-start | bytes 1572872 | tf_op jit(solution)/shard_map/ppermute | solution.py:34
  108.1 25.8 %collective-permute-start.32 = (bf16[4,16,4608]{2,1,0:T(8,128)(2,1)S(1)}, bf16[4,16,4608]{2,1,0:T(8,128)(2,1)S(1)}, u32[]{:S(2)}, u32[]{:S(2)}) collective-permute-start(bf16[4,16,4608]{2,1,0:T(8,128)(2,1)S(1)} %pad_maximum_fusion.refs_0_), channel_id=1, source_target_pairs={{0,1},{1,0},{2,3},{3,2},{4,5},{5,4},{6,7},{7,6},{8,9},{9,8},{10,11... | collective-permute-start | bytes 1769480 | tf_op jit(solution)/shard_map/ppermute | solution.py:34
  108.2 25.7 %collective-permute-start.35 = (bf16[4,16,4608]{2,1,0:T(8,128)(2,1)S(1)}, bf16[4,16,4608]{2,1,0:T(8,128)(2,1)S(1)}, u32[]{:S(2)}, u32[]{:S(2)}) collective-permute-start(bf16[4,16,4608]{2,1,0:T(8,128)(2,1)S(1)} %collective-permute-done.31.refs_3_), channel_id=1, source_target_pairs={{0,1},{1,0},{2,3},{3,2},{4,5},{5,4},{6,7},{7,6},{8,9},{9,8},{10,11... | collective-permute-start | bytes 1769480 | tf_op jit(solution)/shard_map/ppermute | solution.py:34
  108.7 25.2 %collective-permute-start.34 = (bf16[4,16,4608]{2,1,0:T(8,128)(2,1)S(1)}, bf16[4,16,4608]{2,1,0:T(8,128)(2,1)S(1)}, u32[]{:S(2)}, u32[]{:S(2)}) collective-permute-start(bf16[4,16,4608]{2,1,0:T(8,128)(2,1)S(1)} %collective-permute-done.30.refs_2_), channel_id=1, source_target_pairs={{0,1},{1,0},{2,3},{3,2},{4,5},{5,4},{6,7},{7,6},{8,9},{9,8},{10,11... | collective-permute-start | bytes 1769480 | tf_op jit(solution)/shard_map/ppermute | solution.py:34
  108.8 25.2 %collective-permute-start.33 = (bf16[4,16,4608]{2,1,0:T(8,128)(2,1)S(1)}, bf16[4,16,4608]{2,1,0:T(8,128)(2,1)S(1)}, u32[]{:S(2)}, u32[]{:S(2)}) collective-permute-start(bf16[4,16,4608]{2,1,0:T(8,128)(2,1)S(1)} %collective-permute-done.29.refs_1_), channel_id=1, source_target_pairs={{0,1},{1,0},{2,3},{3,2},{4,5},{5,4},{6,7},{7,6},{8,9},{9,8},{10,11... | collective-permute-start | bytes 1769480 | tf_op jit(solution)/shard_map/ppermute | solution.py:34
  227.0 2.6 collective-permute-start.42
  228.5 26.1 %collective-permute-start.36 = (bf16[512,512]{1,0:T(8,128)(2,1)S(1)}, bf16[512,512]{1,0:T(8,128)(2,1)S(1)}, u32[]{:S(2)}, u32[]{:S(2)}) collective-permute-start(bf16[512,512]{1,0:T(8,128)(2,1)S(1)} %get-tuple-element.87), channel_id=1, source_target_pairs={{0,1},{1,0},{2,3},{3,2},{4,5},{5,4},{6,7},{7,6},{8,9},{9,8},{10,11... | collective-permute-start | bytes 1572872 | tf_op jit(solution)/shard_map/ppermute | solution.py:34
  228.9 15.5 %collective-permute-start.37 = (bf16[512,512]{1,0:T(8,128)(2,1)S(1)}, bf16[512,512]{1,0:T(8,128)(2,1)S(1)}, u32[]{:S(2)}, u32[]{:S(2)}) collective-permute-start(bf16[512,512]{1,0:T(8,128)(2,1)S(1)} %get-tuple-element.88), channel_id=1, source_target_pairs={{0,1},{1,0},{2,3},{3,2},{4,5},{5,4},{6,7},{7,6},{8,9},{9,8},{10,11... | collective-permute-start | bytes 1572872 | tf_op jit(solution)/shard_map/ppermute | solution.py:34
  229.9 7.8 %collective-permute-start.43 = (bf16[4,16,1536]{2,1,0:T(8,128)(2,1)S(1)}, bf16[4,16,1536]{2,1,0:T(8,128)(2,1)S(1)}, u32[]{:S(2)}, u32[]{:S(2)}) collective-permute-start(bf16[4,16,1536]{2,1,0:T(8,128)(2,1)S(1)} %get-tuple-element.92), channel_id=1, source_target_pairs={{0,2},{1,3},{2,0},{3,1},{4,6},{5,7},{6,4},{7,5},{8,10},{9,11},{10,... | collective-permute-start | bytes 589832 | tf_op jit(solution)/shard_map/ppermute | solution.py:34
  231.5 9.7 %collective-permute-start.45 = (bf16[4,16,1536]{2,1,0:T(8,128)(2,1)S(1)}, bf16[4,16,1536]{2,1,0:T(8,128)(2,1)S(1)}, u32[]{:S(2)}, u32[]{:S(2)}) collective-permute-start(bf16[4,16,1536]{2,1,0:T(8,128)(2,1)S(1)} %get-tuple-element.93), channel_id=1, source_target_pairs={{0,6},{1,7},{2,4},{3,5},{4,2},{5,3},{6,0},{7,1},{8,14},{9,15},{10,... | collective-permute-start | bytes 589832 | tf_op jit(solution)/shard_map/ppermute | solution.py:34
  232.0 10.6 %collective-permute-start.44 = (bf16[4,16,1536]{2,1,0:T(8,128)(2,1)S(1)}, bf16[4,16,1536]{2,1,0:T(8,128)(2,1)S(1)}, u32[]{:S(2)}, u32[]{:S(2)}) collective-permute-start(bf16[4,16,1536]{2,1,0:T(8,128)(2,1)S(1)} %get-tuple-element.94), channel_id=1, source_target_pairs={{0,4},{1,5},{2,6},{3,7},{4,0},{5,1},{6,2},{7,3},{8,12},{9,13},{10,... | collective-permute-start | bytes 589832 | tf_op jit(solution)/shard_map/ppermute | solution.py:34
  237.7 9.2 %collective-permute-start.40 = (bf16[512,512]{1,0:T(8,128)(2,1)S(1)}, bf16[512,512]{1,0:T(8,128)(2,1)S(1)}, u32[]{:S(2)}, u32[]{:S(2)}) collective-permute-start(bf16[512,512]{1,0:T(8,128)(2,1)S(1)} %get-tuple-element.86), channel_id=1, source_target_pairs={{0,1},{1,0},{2,3},{3,2},{4,5},{5,4},{6,7},{7,6},{8,9},{9,8},{10,11... | collective-permute-start | bytes 1572872 | tf_op jit(solution)/shard_map/ppermute | solution.py:34
  241.2 19.1 %collective-permute-start.49 = (bf16[4,4,16,2176]{3,2,1,0:T(8,128)(2,1)S(1)}, bf16[4,4,16,2176]{3,2,1,0:T(8,128)(2,1)S(1)}, u32[]{:S(2)}, u32[]{:S(2)}) collective-permute-start(bf16[4,4,16,2176]{3,2,1,0:T(8,128)(2,1)S(1)} %copy-done.18), channel_id=1, source_target_pairs={{0,1},{1,0},{2,3},{3,2},{4,5},{5,4},{6,7},{7,6},{8,9},{9,8},{10,11... | collective-permute-start | bytes 3342344 | tf_op jit(solution)/shard_map/ppermute | solution.py:34
  242.7 6.2 %collective-permute-start.46 = (bf16[16,1536]{1,0:T(8,128)(2,1)S(1)}, bf16[16,1536]{1,0:T(8,128)(2,1)S(1)}, u32[]{:S(2)}, u32[]{:S(2)}) collective-permute-start(bf16[16,1536]{1,0:T(8,128)(2,1)S(1)} %get-tuple-element.106), channel_id=1, source_target_pairs={{0,8},{1,9},{2,10},{3,11},{4,12},{5,13},{6,14},{7,15},{8,0},{9,1},... | collective-permute-start | bytes 147464 | tf_op jit(solution)/shard_map/ppermute | solution.py:34
  245.6 13.4 %collective-permute-start.38 = (bf16[512,512]{1,0:T(8,128)(2,1)S(1)}, bf16[512,512]{1,0:T(8,128)(2,1)S(1)}, u32[]{:S(2)}, u32[]{:S(2)}) collective-permute-start(bf16[512,512]{1,0:T(8,128)(2,1)S(1)} %fusion.4), channel_id=1, source_target_pairs={{0,2},{1,3},{2,0},{3,1},{4,6},{5,7},{6,4},{7,5},{8,10},{9,11},{10,... | collective-permute-start | bytes 1572872 | tf_op jit(solution)/shard_map/ppermute | solution.py:34
  246.9 5.9 %collective-permute-start.48 = (bf16[16,1536]{1,0:T(8,128)(2,1)S(1)}, bf16[16,1536]{1,0:T(8,128)(2,1)S(1)}, u32[]{:S(2)}, u32[]{:S(2)}) collective-permute-start(bf16[16,1536]{1,0:T(8,128)(2,1)S(1)} %get-tuple-element.107), channel_id=1, source_target_pairs={{0,24},{1,25},{2,26},{3,27},{4,28},{5,29},{6,30},{7,31},{8,16},{9,... | collective-permute-start | bytes 147464 | tf_op jit(solution)/shard_map/ppermute | solution.py:34
  248.9 5.0 %collective-permute-start.47 = (bf16[16,1536]{1,0:T(8,128)(2,1)S(1)}, bf16[16,1536]{1,0:T(8,128)(2,1)S(1)}, u32[]{:S(2)}, u32[]{:S(2)}) collective-permute-start(bf16[16,1536]{1,0:T(8,128)(2,1)S(1)} %get-tuple-element.108), channel_id=1, source_target_pairs={{0,16},{1,17},{2,18},{3,19},{4,20},{5,21},{6,22},{7,23},{8,24},{9,... | collective-permute-start | bytes 147464 | tf_op jit(solution)/shard_map/ppermute | solution.py:34
  252.8 10.8 %collective-permute-start.39 = (bf16[512,512]{1,0:T(8,128)(2,1)S(1)}, bf16[512,512]{1,0:T(8,128)(2,1)S(1)}, u32[]{:S(2)}, u32[]{:S(2)}) collective-permute-start(bf16[512,512]{1,0:T(8,128)(2,1)S(1)} %get-tuple-element.85), channel_id=1, source_target_pairs={{0,1},{1,0},{2,3},{3,2},{4,5},{5,4},{6,7},{7,6},{8,9},{9,8},{10,11... | collective-permute-start | bytes 1572872 | tf_op jit(solution)/shard_map/ppermute | solution.py:34
  253.9 32.0 %collective-permute-start.56 = (bf16[4,4,16,4608]{3,2,1,0:T(8,128)(2,1)S(1)}, bf16[4,4,16,4608]{3,2,1,0:T(8,128)(2,1)S(1)}, u32[]{:S(2)}, u32[]{:S(2)}) collective-permute-start(bf16[4,4,16,4608]{3,2,1,0:T(8,128)(2,1)S(1)} %copy-done.17), channel_id=1, source_target_pairs={{0,1},{1,0},{2,3},{3,2},{4,5},{5,4},{6,7},{7,6},{8,9},{9,8},{10,11... | collective-permute-start | bytes 7077896 | tf_op jit(solution)/shard_map/ppermute | solution.py:34
  254.6 15.7 %collective-permute-start.41 = (bf16[512,512]{1,0:T(8,128)(2,1)S(1)}, bf16[512,512]{1,0:T(8,128)(2,1)S(1)}, u32[]{:S(2)}, u32[]{:S(2)}) collective-permute-start(bf16[512,512]{1,0:T(8,128)(2,1)S(1)} %fusion.3), channel_id=1, source_target_pairs={{0,2},{1,3},{2,0},{3,1},{4,6},{5,7},{6,4},{7,5},{8,10},{9,11},{10,... | collective-permute-start | bytes 1572872 | tf_op jit(solution)/shard_map/ppermute | solution.py:34
  260.9 15.4 %collective-permute-start.50 = (bf16[4,16,2176]{2,1,0:T(8,128)(2,1)S(1)}, bf16[4,16,2176]{2,1,0:T(8,128)(2,1)S(1)}, u32[]{:S(2)}, u32[]{:S(2)}) collective-permute-start(bf16[4,16,2176]{2,1,0:T(8,128)(2,1)S(1)} %get-tuple-element.89), channel_id=1, source_target_pairs={{0,2},{1,3},{2,0},{3,1},{4,6},{5,7},{6,4},{7,5},{8,10},{9,11},{10,... | collective-permute-start | bytes 835592 | tf_op jit(solution)/shard_map/ppermute | solution.py:34
  262.5 19.7 %collective-permute-start.52 = (bf16[4,16,2176]{2,1,0:T(8,128)(2,1)S(1)}, bf16[4,16,2176]{2,1,0:T(8,128)(2,1)S(1)}, u32[]{:S(2)}, u32[]{:S(2)}) collective-permute-start(bf16[4,16,2176]{2,1,0:T(8,128)(2,1)S(1)} %get-tuple-element.90), channel_id=1, source_target_pairs={{0,6},{1,7},{2,4},{3,5},{4,2},{5,3},{6,0},{7,1},{8,14},{9,15},{10,... | collective-permute-start | bytes 835592 | tf_op jit(solution)/shard_map/ppermute | solution.py:34
  263.6 18.7 %collective-permute-start.51 = (bf16[4,16,2176]{2,1,0:T(8,128)(2,1)S(1)}, bf16[4,16,2176]{2,1,0:T(8,128)(2,1)S(1)}, u32[]{:S(2)}, u32[]{:S(2)}) collective-permute-start(bf16[4,16,2176]{2,1,0:T(8,128)(2,1)S(1)} %get-tuple-element.91), channel_id=1, source_target_pairs={{0,4},{1,5},{2,6},{3,7},{4,0},{5,1},{6,2},{7,3},{8,12},{9,13},{10,... | collective-permute-start | bytes 835592 | tf_op jit(solution)/shard_map/ppermute | solution.py:34
  282.4 7.6 %collective-permute-start.53 = (bf16[16,2176]{1,0:T(8,128)(2,1)S(1)}, bf16[16,2176]{1,0:T(8,128)(2,1)S(1)}, u32[]{:S(2)}, u32[]{:S(2)}) collective-permute-start(bf16[16,2176]{1,0:T(8,128)(2,1)S(1)} %get-tuple-element.103), channel_id=1, source_target_pairs={{0,8},{1,9},{2,10},{3,11},{4,12},{5,13},{6,14},{7,15},{8,0},{9,1},... | collective-permute-start | bytes 208904 | tf_op jit(solution)/shard_map/ppermute | solution.py:34
  283.3 7.9 %collective-permute-start.55 = (bf16[16,2176]{1,0:T(8,128)(2,1)S(1)}, bf16[16,2176]{1,0:T(8,128)(2,1)S(1)}, u32[]{:S(2)}, u32[]{:S(2)}) collective-permute-start(bf16[16,2176]{1,0:T(8,128)(2,1)S(1)} %get-tuple-element.104), channel_id=1, source_target_pairs={{0,24},{1,25},{2,26},{3,27},{4,28},{5,29},{6,30},{7,31},{8,16},{9,... | collective-permute-start | bytes 208904 | tf_op jit(solution)/shard_map/ppermute | solution.py:34
  285.6 6.5 %collective-permute-start.54 = (bf16[16,2176]{1,0:T(8,128)(2,1)S(1)}, bf16[16,2176]{1,0:T(8,128)(2,1)S(1)}, u32[]{:S(2)}, u32[]{:S(2)}) collective-permute-start(bf16[16,2176]{1,0:T(8,128)(2,1)S(1)} %get-tuple-element.105), channel_id=1, source_target_pairs={{0,16},{1,17},{2,18},{3,19},{4,20},{5,21},{6,22},{7,23},{8,24},{9,... | collective-permute-start | bytes 208904 | tf_op jit(solution)/shard_map/ppermute | solution.py:34
  287.7 16.6 %collective-permute-start.57 = (bf16[4,16,4608]{2,1,0:T(8,128)(2,1)}, bf16[4,16,4608]{2,1,0:T(8,128)(2,1)}, u32[]{:S(2)}, u32[]{:S(2)}) collective-permute-start(bf16[4,16,4608]{2,1,0:T(8,128)(2,1)} %get-tuple-element.82), channel_id=1, source_target_pairs={{0,2},{1,3},{2,0},{3,1},{4,6},{5,7},{6,4},{7,5},{8,10},{9,11},{10,... | collective-permute-start | bytes 1769480 | tf_op jit(solution)/shard_map/ppermute | solution.py:34
  289.2 25.7 %collective-permute-start.59 = (bf16[4,16,4608]{2,1,0:T(8,128)(2,1)S(1)}, bf16[4,16,4608]{2,1,0:T(8,128)(2,1)}, u32[]{:S(2)}, u32[]{:S(2)}) collective-permute-start(bf16[4,16,4608]{2,1,0:T(8,128)(2,1)S(1)} %get-tuple-element.83), channel_id=1, source_target_pairs={{0,6},{1,7},{2,4},{3,5},{4,2},{5,3},{6,0},{7,1},{8,14},{9,15},{10,... | collective-permute-start | bytes 1769480 | tf_op jit(solution)/shard_map/ppermute | solution.py:34
  290.0 26.0 %collective-permute-start.58 = (bf16[4,16,4608]{2,1,0:T(8,128)(2,1)S(1)}, bf16[4,16,4608]{2,1,0:T(8,128)(2,1)}, u32[]{:S(2)}, u32[]{:S(2)}) collective-permute-start(bf16[4,16,4608]{2,1,0:T(8,128)(2,1)S(1)} %get-tuple-element.84), channel_id=1, source_target_pairs={{0,4},{1,5},{2,6},{3,7},{4,0},{5,1},{6,2},{7,3},{8,12},{9,13},{10,... | collective-permute-start | bytes 1769480 | tf_op jit(solution)/shard_map/ppermute | solution.py:34
  317.8 5.4 %collective-permute-start.60 = (bf16[16,4608]{1,0:T(8,128)(2,1)S(1)}, bf16[16,4608]{1,0:T(8,128)(2,1)S(1)}, u32[]{:S(2)}, u32[]{:S(2)}) collective-permute-start(bf16[16,4608]{1,0:T(8,128)(2,1)S(1)} %get-tuple-element.95), channel_id=1, source_target_pairs={{0,8},{1,9},{2,10},{3,11},{4,12},{5,13},{6,14},{7,15},{8,0},{9,1},... | collective-permute-start | bytes 442376 | tf_op jit(solution)/shard_map/ppermute | solution.py:34
  319.1 7.0 %collective-permute-start.62 = (bf16[16,4608]{1,0:T(8,128)(2,1)S(1)}, bf16[16,4608]{1,0:T(8,128)(2,1)S(1)}, u32[]{:S(2)}, u32[]{:S(2)}) collective-permute-start(bf16[16,4608]{1,0:T(8,128)(2,1)S(1)} %get-tuple-element.96), channel_id=1, source_target_pairs={{0,24},{1,25},{2,26},{3,27},{4,28},{5,29},{6,30},{7,31},{8,16},{9,... | collective-permute-start | bytes 442376 | tf_op jit(solution)/shard_map/ppermute | solution.py:34
  321.1 9.7 %collective-permute-start.61 = (bf16[16,4608]{1,0:T(8,128)(2,1)S(1)}, bf16[16,4608]{1,0:T(8,128)(2,1)S(1)}, u32[]{:S(2)}, u32[]{:S(2)}) collective-permute-start(bf16[16,4608]{1,0:T(8,128)(2,1)S(1)} %get-tuple-element.97), channel_id=1, source_target_pairs={{0,16},{1,17},{2,18},{3,19},{4,20},{5,21},{6,22},{7,23},{8,24},{9,... | collective-permute-start | bytes 442376 | tf_op jit(solution)/shard_map/ppermute | solution.py:34
  (29 other events, 629.9 us)
